TPU v7x, 32 devices: a whole 2x2x4 slice. The times are simulated.
32 devices in a mesh: groups: 1, dp: 16 (over z, y, core), tp: 2 (over x).
Axes of the slice: x: 2, y: 2, z: 4, core: 2. Of those that a mesh axis runs over, the one named last changes fastest.
Arguments:
- latent_cache: bfloat16 [32, 32, 576], P(('groups', 'dp')), may hold values from -6 to 6
- lengths: int32 [32], P('groups'), may hold values from 2 to 30
- destination: int32 [32], P('groups'), may hold values from 0 to 15, as said below
- queries: bfloat16 [32, 2, 64, 576], P(('groups', 'dp'), None, 'tp'), may hold values from -21 to 21
- new_latent: bfloat16 [32, 2, 576], P(('groups', 'dp')), may hold values from -6 to 6
- residual: bfloat16 [32, 2, 3584], P('groups', None, 'dp'), may hold values from -4 to 4
- w_out: bfloat16 [64, 512, 3584], P('tp', None, 'dp'), may hold values from -0.09375 to 0.09375
- norm_gain: float32 [3584], replicated, may hold values from 0.1 to 1.9
- w_gate: bfloat16 [16, 3584, 1024], P('dp', None, 'tp'), may hold values from -0.09375 to 0.09375
- w_up: bfloat16 [16, 3584, 1024], P('dp', None, 'tp'), may hold values from -0.09375 to 0.09375
- w_down: bfloat16 [16, 1024, 3584], P('dp', 'tp'), may hold values from -0.1875 to 0.1875
- experts: int32 [32, 2, 8], P('groups'), may hold values from 0 to 15, all different within a row; in each aligned block of 4 rows (0 to 3, 4 to 7, ..., all dimensions but the last counted through in order) at most 4 rows name the same one
- gate_weights: float32 [32, 2, 8], P('groups'), may hold values from 0.05 to 0.5
Outputs:
- layer_out: bfloat16 [32, 2, 3584], P('groups', None, ('dp', 'tp'))
Inputs may be any that keep to these rules, and one draw needn't show every extreme that they name: `destination`: A request keeps its slot index. For each slot index the destinations of the 16 ranks' requests are a permutation of the ranks; no rank sends more than 1 request to one rank, and some rank sends exactly 1 to one rank. Each token names 8 different experts. In the rows of one rank (2 requests times 2 steps, in order) no expert is named more than 4 times, a bound that some block reaches.
All inputs are finite; a program needn't handle non-finite values.
Results may differ from a plain program's by a relative error of at most 0.014.
Values may be sent and summed in bfloat16 or wider, within the bound.
No kernel may reach another device: no remote copies, remote signals or barrier semaphores. Data moves between devices by JAX's collectives and lax.ppermute only.
A program may use at most 128 MiB of HBM per device.

v0:
```python
import jax
import jax.numpy as jnp
from jax import lax
from jax.sharding import PartitionSpec as P

score_scale = 192.0 ** (-0.5)
norm_eps = 1e-06


def expert_slots(experts, block_count, expert_count, capacity):
    flat_ids = experts.reshape(block_count, -1)
    onehot = (
        flat_ids[:, :, None] == jnp.arange(expert_count, dtype=jnp.int32)[None, None, :]
    ).astype(jnp.int32)
    before = jnp.cumsum(onehot, axis=1) - onehot
    within = jnp.sum(onehot * before, axis=-1)
    position_in = jnp.arange(block_count, dtype=jnp.int32)[:, None] * capacity + within
    return (position_in.reshape(-1), flat_ids.reshape(-1))


def attend(queries, full_cache, visible, latent_width):
    scores = (
        jnp.einsum("stha,spa->sthp", queries, full_cache, preferred_element_type=jnp.float32)
        * score_scale
    )
    scores = jnp.where(visible[:, :, None, :], scores, -1e30)
    highest = jnp.max(scores, axis=-1, keepdims=True)
    raised = jnp.exp(scores - highest)
    weights = (raised / jnp.sum(raised, axis=-1, keepdims=True)).astype(jnp.bfloat16)
    return jnp.einsum(
        "sthp,spl->sthl",
        weights,
        full_cache[..., :latent_width],
        preferred_element_type=jnp.float32,
    ).astype(jnp.bfloat16)


def body(
    latent_cache,
    lengths,
    destination,
    queries,
    new_latent,
    residual,
    w_out,
    norm_gain,
    w_gate,
    w_up,
    w_down,
    experts,
    gate_weights,
):
    ranks = lax.axis_size("dp")
    tp_width = lax.axis_size("tp")
    rank_here = lax.axis_index("dp")
    tp_here = lax.axis_index("tp")
    slot_count, positions, latent_all = latent_cache.shape
    heads_here, latent_width, column_count = w_out.shape
    step_count = queries.shape[1]
    move_room = (slot_count + ranks - 1) // ranks
    slot_range = jnp.arange(slot_count, dtype=jnp.int32)
    routing = destination.reshape(ranks, slot_count)
    own_targets = lax.dynamic_index_in_dim(routing, rank_here, 0, keepdims=False)
    earlier_same = (own_targets[:, None] == own_targets[None, :]) & (
        slot_range[:, None] > slot_range[None, :]
    )
    send_order = jnp.sum(earlier_same.astype(jnp.int32), axis=1)
    buffer_rows = jnp.arange(ranks * move_room, dtype=jnp.int32)
    selector = (
        (own_targets[None, :] == buffer_rows[:, None] // move_room)
        & (send_order[None, :] == buffer_rows[:, None] % move_room)
    ).astype(jnp.bfloat16)
    arrivals = (routing == rank_here).astype(jnp.int32)
    source_rank = jnp.sum(arrivals * jnp.arange(ranks, dtype=jnp.int32)[:, None], axis=0)
    before_here = jnp.cumsum(arrivals, axis=1) - arrivals
    recv_order = jnp.sum(arrivals * before_here, axis=0)
    landing = source_rank * move_room + recv_order
    packed = jnp.dot(
        selector,
        latent_cache.reshape(slot_count, positions * latent_all),
        preferred_element_type=jnp.float32,
    ).astype(jnp.bfloat16)
    arrived = lax.all_to_all(
        packed.reshape(ranks, move_room, positions, latent_all),
        "dp",
        split_axis=0,
        concat_axis=0,
        tiled=True,
    )
    moved = arrived.reshape(ranks * move_room, positions, latent_all)[landing]
    moved_len = lengths[source_rank * slot_count + slot_range]
    position_range = jnp.arange(positions, dtype=jnp.int32)
    full_cache = moved
    for step_index in range(step_count):
        writing = position_range[None, :] == (moved_len + step_index)[:, None]
        full_cache = jnp.where(
            writing[:, :, None], new_latent[:, step_index][:, None, :], full_cache
        )
    visible = (
        position_range[None, None, :]
        < (moved_len[:, None] + jnp.arange(step_count, dtype=jnp.int32)[None, :] + 1)[:, :, None]
    )
    attended = attend(queries, full_cache, visible, latent_width)
    flat_attended = attended.reshape(slot_count * step_count, heads_here * latent_width)
    out_matrix = w_out.reshape(heads_here * latent_width, column_count)
    all_attended = lax.all_gather(flat_attended, "dp", axis=0, tiled=True)
    head_partial = jnp.dot(all_attended, out_matrix, preferred_element_type=jnp.float32)
    attn_cols = lax.psum(head_partial.astype(jnp.bfloat16), "tp").astype(jnp.float32)
    row_total = residual.shape[0] * residual.shape[1]
    mixed = (residual.reshape(row_total, column_count).astype(jnp.float32) + attn_cols).astype(
        jnp.bfloat16
    )
    top_count = experts.shape[2]
    block_rows = slot_count * step_count
    capacity = min(block_rows, max(8, 3 * block_rows * top_count // (2 * ranks)))
    slot_room = ranks * capacity
    position_in, expert_flat = expert_slots(experts, ranks, ranks, capacity)
    row_ids = jnp.arange(row_total * top_count, dtype=jnp.int32) // top_count
    sender_table = (
        jnp.full((ranks * slot_room,), -1, jnp.int32)
        .at[expert_flat * slot_room + position_in]
        .set(row_ids)
    )
    outgoing = jnp.where((sender_table >= 0)[:, None], mixed[jnp.maximum(sender_table, 0)], 0)
    outgoing = outgoing.reshape(ranks, slot_room, column_count)
    rows_in = lax.all_to_all(outgoing, "dp", split_axis=0, concat_axis=2, tiled=True)
    rows_wide = rows_in[0].astype(jnp.float32)
    inverse_rms = lax.rsqrt(jnp.mean(rows_wide * rows_wide, axis=-1, keepdims=True) + norm_eps)
    normed = (rows_wide * inverse_rms * norm_gain).astype(jnp.bfloat16)
    gate_proj = jnp.dot(normed, w_gate[0], preferred_element_type=jnp.float32)
    up_proj = jnp.dot(normed, w_up[0], preferred_element_type=jnp.float32)
    activated = (jax.nn.silu(gate_proj) * up_proj).astype(jnp.bfloat16)
    expert_terms = jnp.dot(activated, w_down[0], preferred_element_type=jnp.float32)
    share = column_count // tp_width
    laid_out = expert_terms.reshape(slot_room, ranks, tp_width, share)
    arrived_terms = lax.all_to_all(
        lax.all_to_all(
            laid_out.astype(jnp.bfloat16), "dp", split_axis=1, concat_axis=1, tiled=True
        ),
        "tp",
        split_axis=2,
        concat_axis=2,
        tiled=True,
    )
    returned = jnp.sum(arrived_terms.astype(jnp.float32), axis=2)
    collected = returned.reshape(slot_room * ranks, share)
    picked = collected[position_in * ranks + expert_flat].reshape(row_total, top_count, share)
    moe_part = jnp.sum(gate_weights.reshape(row_total, top_count)[:, :, None] * picked, axis=1)
    own_columns = lax.dynamic_slice_in_dim(mixed, tp_here * share, share, 1)
    return (
        (own_columns.astype(jnp.float32) + moe_part)
        .astype(jnp.bfloat16)
        .reshape(residual.shape[0], step_count, share)
    )


def solution(mesh):
    placed = (
        P(("groups", "dp"), None, None),
        P("groups"),
        P("groups"),
        P(("groups", "dp"), None, "tp", None),
        P(("groups", "dp"), None, None),
        P("groups", None, "dp"),
        P("tp", None, "dp"),
        P(),
        P("dp", None, "tp"),
        P("dp", None, "tp"),
        P("dp", "tp", None),
        P("groups", None, None),
        P("groups", None, None),
    )
    return jax.shard_map(
        body, mesh=mesh, in_specs=placed, out_specs=P("groups", None, ("dp", "tp")), check_vma=False
    )
```

profile of v0, /device:TPU:0, one launch (start us, length us, event | category | flops | bytes accessed | tf_op | source)
XLA Modules:
  0.0 167.3 jit_solution(3646099686042609234)
XLA Ops:
  6.5 0.8 reshape.299
  7.3 0.2 fusion.45
  7.5 1.0 reshape.300
  8.6 0.3 convolution_convert_fusion
  8.9 1.6 reshape.301
  10.5 7.4 %all-to-all-start = ((bf16[16,1,32,576]{3,2,1,0:T(8,128)(2,1)}), bf16[16,1,32,576]{3,2,1,0:T(8,128)(2,1)S(1)}, u32[]{:S(2)}, u32[]{:S(2)}) async-start(bf16[16,1,32,576]{3,2,1,0:T(8,128)(2,1)} %bitcast.3), calls=%async_computation | async-start | bytes 1310720 | tf_op jit(solution)/shard_map/all_to_all | solution.py:83
  17.9 0.2 reduce_window_sum.22
  18.2 0.6 gather_fusion
  18.9 0.1 iota_compare_fusion.4
  19.1 15.4 %all-to-all-done = bf16[16,1,32,576]{3,2,1,0:T(8,128)(2,1)S(1)} async-done(((bf16[16,1,32,576]{3,2,1,0:T(8,128)(2,1)}), bf16[16,1,32,576]{3,2,1,0:T(8,128)(2,1)S(1)}, u32[]{:S(2)}, u32[]{:S(2)}) %all-to-all-start) | async-done | bytes 589856 | tf_op jit(solution)/shard_map/all_to_all | solution.py:83
  34.5 0.6 gather_fusion.1
  35.0 0.1 select_select_fusion
  35.1 0.3 fusion.15
  35.5 0.2 convolution_convert_fusion.2
  35.7 0.7 reshape.351
  36.5 0.1 copy.63
  36.6 0.1 eq.117
  36.7 0.1 reshape_reshape.3
  36.8 7.0 %copy.79 = bf16[32,28,8,512]{3,2,0,1:T(8,128)(2,1)} copy(bf16[32,28,8,512]{3,2,1,0:T(8,128)(2,1)} %bitcast.91) | data formatting | bytes 14680064 | tf_op jit(solution)/shard_map/reshape | solution.py:105
  43.9 0.8 fusion.53
  44.9 0.1 add.195
  45.0 2.4 %scatter_custom_fusion = s32[1024]{0:T(1024)S(1)} fusion(s32[512]{0:T(512)S(1)} %bitcast.96, s32[512]{0:T(512)S(1)} %add_select_fusion, s32[]{:T(128)} %constant.96.clone.1), kind=kCustom, calls=%fused_computation.75 | custom fusion | bytes 4100 | tf_op jit(solution)/shard_map/scatter | solution.py:122
  47.5 0.1 broadcast_in_dim.102
  47.5 30.5 %all-gather.3.cloned.1.call-done = bf16[16,4,16384]{2,1,0:T(4,128)(2,1)} async-done(((bf16[1,4,16384]{2,1,0:T(4,128)(2,1)}), bf16[16,4,16384]{2,1,0:T(4,128)(2,1)}) %all-gather.3.cloned.1.call-update) | async-done | bytes 2097168 | tf_op jit(solution)/shard_map/all_gather | solution.py:106
  78.0 2.5 %reshape.352 = bf16[64,16384]{1,0:T(8,128)(2,1)S(1)} reshape(bf16[16,4,16384]{2,1,0:T(4,128)(2,1)} %all-gather.3.cloned.1.call-done) | data formatting | bytes 4194304
  80.6 5.5 %convolution_convert_fusion.3 = bf16[64,224]{1,0:T(8,128)(2,1)S(1)} fusion(bf16[64,16384]{1,0:T(8,128)(2,1)S(1)} %reshape.352, bf16[16384,224]{0,1:T(8,128)(2,1)} %bitcast.88), kind=kOutput, calls=%fused_computation.25 | convolution fusion | flops 469776384 | bytes 9465856 | tf_op jit(solution)/shard_map/dot_general | solution.py:107
  86.1 8.5 %psum.7 = bf16[64,224]{1,0:T(8,128)(2,1)S(1)} all-reduce(bf16[64,224]{1,0:T(8,128)(2,1)S(1)} %convolution_convert_fusion.3), channel_id=1, replica_groups=mesh['groups'=1,'dp'=16,'tp'=2] {'tp'}, use_global_device_ids=true, to_apply=%region_6.7 | all-reduce | flops 14336 | bytes 57344 | tf_op jit(solution)/shard_map/psum | solution.py:108
  94.6 3.9 %gather_fusion.2 = bf16[1024,224]{1,0:T(8,128)(2,1)S(1)} fusion(bf16[64,224]{1,0:T(8,128)(2,1)S(1)} %add_convert_fusion, s32[1024]{0:T(1024)S(1)} %maximum_clamp_fusion), kind=kCustom, calls=%fused_computation.2 | custom fusion | bytes 921600 | tf_op jit(solution)/shard_map/gather | solution.py:124
  98.5 1.0 broadcast_select_fusion
  99.5 3.6 %all-to-all-start.1 = ((bf16[16,64,224]{2,1,0:T(8,128)(2,1)}), bf16[16,64,224]{2,1,0:T(8,128)(2,1)S(1)}, u32[]{:S(2)}, u32[]{:S(2)}) async-start(bf16[16,64,224]{2,1,0:T(8,128)(2,1)} %broadcast_select_fusion), calls=%async_computation.1 | async-start | bytes 1048576 | tf_op jit(solution)/shard_map/all_to_all | solution.py:126
  103.2 5.9 %copy.68 = bf16[1,512,3584]{1,2,0:T(8,128)(2,1)} copy(bf16[1,512,3584]{2,1,0:T(8,128)(2,1)} %param.23) | data formatting | bytes 7340032 | tf_op args[10]
  109.1 8.4 %all-to-all-done.1 = bf16[16,64,224]{2,1,0:T(8,128)(2,1)S(1)} async-done(((bf16[16,64,224]{2,1,0:T(8,128)(2,1)}), bf16[16,64,224]{2,1,0:T(8,128)(2,1)S(1)}, u32[]{:S(2)}, u32[]{:S(2)}) %all-to-all-start.1) | async-done | bytes 458784 | tf_op jit(solution)/shard_map/all_to_all | solution.py:126
  117.5 0.2 fusion.19
  117.8 0.2 fusion.24
  118.0 0.3 copy.67
  118.3 0.9 convert_element_type.87
  119.1 2.8 %fusion.3 = f32[64,512]{1,0:T(8,128)S(1)} fusion(bf16[64,3584]{1,0:T(8,128)(2,1)S(1)} %convert_element_type.87, bf16[1,3584,512]{2,1,0:T(8,128)(2,1)} %param.21), kind=kOutput, calls=%fused_computation.9 | convolution fusion | flops 234881024 | bytes 4259840 | tf_op jit(solution)/shard_map/dot_general | solution.py:130
  121.9 5.2 %convolution_convert_fusion.1 = bf16[64,16,2,112]{3,0,2,1:T(8,128)(2,1)S(1)} fusion(bf16[16,2,112,512]{3,2,1,0:T(8,128)(2,1)} %bitcast.89, bf16[64,3584]{1,0:T(8,128)(2,1)S(1)} %convert_element_type.87, bf16[1,3584,512]{2,1,0:T(8,128)(2,1)} %param.22, f32[64,512]{1,0:T(8,128)S(1)} %fusion.3), kind=kOutput, calls=%fused_computation.13 | convolution fusion | flops 470188032 | bytes 8388608 | tf_op jit(solution)/shard_map/dot_general | solution.py:133
  127.1 18.3 %all_to_all.24 = bf16[64,16,2,112]{3,0,2,1:T(8,128)(2,1)S(1)} all-to-all(bf16[64,16,2,112]{3,0,2,1:T(8,128)(2,1)S(1)} %convolution_convert_fusion.1), channel_id=1, replica_groups=mesh['groups'=1,'dp'=16,'tp'=2] {'dp'}, dimensions={1} | all-to-all | bytes 917504 | tf_op jit(solution)/shard_map/all_to_all | solution.py:137
  145.4 0.8 copy.69
  146.2 3.5 %all-to-all-start.3 = ((bf16[64,16,2,112]{3,0,1,2:T(8,128)(2,1)}), bf16[64,16,2,112]{3,0,1,2:T(8,128)(2,1)S(1)}, u32[]{:S(2)}, u32[]{:S(2)}) async-start(bf16[64,16,2,112]{3,0,1,2:T(8,128)(2,1)} %copy.69), calls=%async_computation.3 | async-start | bytes 1048576 | tf_op jit(solution)/shard_map/all_to_all | solution.py:136
  149.7 0.1 copy.62
  149.8 8.3 %all-to-all-done.3 = bf16[64,16,2,112]{3,0,1,2:T(8,128)(2,1)S(1)} async-done(((bf16[64,16,2,112]{3,0,1,2:T(8,128)(2,1)}), bf16[64,16,2,112]{3,0,1,2:T(8,128)(2,1)S(1)}, u32[]{:S(2)}, u32[]{:S(2)}) %all-to-all-start.3) | async-done | bytes 458784 | tf_op jit(solution)/shard_map/all_to_all | solution.py:136
  158.1 0.1 convert_reduce_fusion
  158.2 0.3 copy.71
  158.6 1.0 gather_fusion.3
  159.6 0.1 fusion.25
  159.8 0.7 add_convert_fusion.1
  (42 shorter events, 0.7 us)
Async XLA Ops:
  6.5 28.6 %copy-start = (bf16[2,2,32,576]{3,2,1,0:T(8,128)(2,1)S(1)}, bf16[2,2,32,576]{3,2,1,0:T(8,128)(2,1)}, u32[]{:S(2)}) copy-start(bf16[2,2,32,576]{3,2,1,0:T(8,128)(2,1)} %param.16) | copy-start | bytes 442372
  6.5 11.6 %copy-start.1 = (s32[32]{0:T(128)S(1)}, s32[32]{0:T(128)}, u32[]{:S(2)}) copy-start(s32[32]{0:T(128)} %param.14) | copy-start | bytes 388
  6.5 12.5 %copy-start.3 = (bf16[2,2,576]{2,1,0:T(2,128)(2,1)S(1)}, bf16[2,2,576]{2,1,0:T(2,128)(2,1)}, u32[]{:S(2)}) copy-start(bf16[2,2,576]{2,1,0:T(2,128)(2,1)} %param.17) | copy-start | bytes 13828
  6.5 29.9 %copy-start.5 = (s32[32,2,8]{0,2,1:T(8,128)S(1)}, s32[32,2,8]{0,2,1:T(8,128)}, u32[]{:S(2)}) copy-start(s32[32,2,8]{0,2,1:T(8,128)} %param.24) | copy-start | bytes 6148
  10.5 24.0 %all-to-all-start = ((bf16[16,1,32,576]{3,2,1,0:T(8,128)(2,1)}), bf16[16,1,32,576]{3,2,1,0:T(8,128)(2,1)S(1)}, u32[]{:S(2)}, u32[]{:S(2)}) async-start(bf16[16,1,32,576]{3,2,1,0:T(8,128)(2,1)} %bitcast.3), calls=%async_computation | async-start | bytes 1310720 | tf_op jit(solution)/shard_map/all_to_all | solution.py:83
  17.9 60.2 %all-gather.3.cloned.1.call-start = ((), (), s32[]{:S(2)}) async-start(), calls=%async_computation.4 | async-start | bytes 2228224 | tf_op jit(solution)/shard_map/all_gather | solution.py:106
  36.8 7.0 %copy-start.2 = (bf16[32,2,224]{2,1,0:T(2,128)(2,1)S(1)}, bf16[32,2,224]{2,1,0:T(2,128)(2,1)}, u32[]{:S(2)}) copy-start(bf16[32,2,224]{2,1,0:T(2,128)(2,1)} %param.18) | copy-start | bytes 86020
  86.1 17.0 %copy-start.4 = (f32[3584]{0:T(1024)S(1)}, f32[3584]{0:T(1024)}, u32[]{:S(2)}) copy-start(f32[3584]{0:T(1024)} %param.20) | copy-start | bytes 43012
  99.5 18.0 %all-to-all-start.1 = ((bf16[16,64,224]{2,1,0:T(8,128)(2,1)}), bf16[16,64,224]{2,1,0:T(8,128)(2,1)S(1)}, u32[]{:S(2)}, u32[]{:S(2)}) async-start(bf16[16,64,224]{2,1,0:T(8,128)(2,1)} %broadcast_select_fusion), calls=%async_computation.1 | async-start | bytes 1048576 | tf_op jit(solution)/shard_map/all_to_all | solution.py:126
  121.9 27.8 %copy-start.6 = (f32[32,2,8]{0,2,1:T(8,128)S(1)}, f32[32,2,8]{0,2,1:T(8,128)}, u32[]{:S(2)}) copy-start(f32[32,2,8]{0,2,1:T(8,128)} %param.25) | copy-start | bytes 6148
  146.2 11.9 %all-to-all-start.3 = ((bf16[64,16,2,112]{3,0,1,2:T(8,128)(2,1)}), bf16[64,16,2,112]{3,0,1,2:T(8,128)(2,1)S(1)}, u32[]{:S(2)}, u32[]{:S(2)}) async-start(bf16[64,16,2,112]{3,0,1,2:T(8,128)(2,1)} %copy.69), calls=%async_computation.3 | async-start | bytes 1048576 | tf_op jit(solution)/shard_map/all_to_all | solution.py:136
Sparse Core Ops, SparseCore 0:
  36.6 41.4 all-gather.2
where the time goes:
time: 168 us; the launch traced here: 167 us
  waiting for transfers between devices  62.6 us (37%)
  local copies, waits for them, and re-layouts  31.4 us (19%)
  blocking collectives  26.8 us (16%)
  starting transfers between devices  14.5 us (9%)
  matrix products  14.2 us (8%)
  between operations  13.7 us (8%)
  other arithmetic  4.13 us (2%)
    all_gather x1, waiting for transfers between devices, body(): all_attended = lax.all_gather(flat_attended, 'dp', axis=0, tiled=True)  30.5 us
    all_to_all x1, blocking collectives, body(): lax.all_to_all(laid_out.astype(jnp.bfloat16), 'dp', split_axis=1, concat_...  18.3 us
    all_to_all x1, waiting for transfers between devices, body(): lax.all_to_all(packed.reshape(ranks, move_room, positions, latent_all), '...  15.4 us
    unnamed x20, local copies, waits for them, and re-layouts  9.4 us
    psum x1, blocking collectives, body(): lax.psum(head_partial.astype(jnp.bfloat16), 'tp').astype(jnp.float32)  8.46 us
    all_to_all x1, waiting for transfers between devices, body(): lax.all_to_all(outgoing, 'dp', split_axis=0, concat_axis=2, tiled=True)  8.42 us
    all_to_all x1, waiting for transfers between devices, body(): lax.all_to_all(lax.all_to_all(laid_out.astype(jnp.bfloat16), 'dp', split_...  8.3 us
    all_to_all x1, starting transfers between devices, body(): lax.all_to_all(packed.reshape(ranks, move_room, positions, latent_all), '...  7.39 us
  transfers between devices with their start and end apart: 4, of which 4 were waited for; matrix products, arithmetic and copies ran while one was open for 11% of the time, Pallas kernels for 0%

commit v1 on v0

v1 whole, which is shorter than its diff:
```python
import jax
import jax.numpy as jnp
from jax import lax
from jax.sharding import Mesh, PartitionSpec as P

score_scale = 192.0 ** (-0.5)
norm_eps = 1e-06


def swap_core(x):
    return lax.ppermute(x, "core", [(0, 1), (1, 0)])


def swap_chip(x, bits):
    count = lax.axis_size("chip")
    return lax.ppermute(x, "chip", [(i, i ^ bits) for i in range(count)])


def swap_tp(x, bits):
    count = lax.axis_size("tp")
    return lax.ppermute(x, "tp", [(i, i ^ bits) for i in range(count)])


def gather_relative(x):
    chips = lax.axis_size("chip")
    far = jnp.stack([x] + [swap_chip(x, 2 * k) for k in range(1, chips // 2)])
    near = jnp.stack([far, swap_chip(far, 1)])
    return jnp.stack([near, swap_core(near)])


def gather_equal(x, axes, count):
    spread = jnp.broadcast_to(x[None], (count,) + x.shape)
    return lax.all_to_all(spread, axes, 0, 0, tiled=True)


def body(
    latent_cache,
    lengths,
    destination,
    queries,
    new_latent,
    residual,
    w_out,
    norm_gain,
    w_gate,
    w_up,
    w_down,
    experts,
    gate_weights,
):
    chips = lax.axis_size("chip")
    tp_width = lax.axis_size("tp")
    ranks = chips * 2
    chip_here = lax.axis_index("chip")
    core_here = lax.axis_index("core")
    tp_here = lax.axis_index("tp")
    rank_here = chip_here * 2 + core_here
    slot_count, positions, latent_all = latent_cache.shape
    heads_here, latent_width, column_count = w_out.shape
    step_count = queries.shape[1]
    block_rows = slot_count * step_count
    row_total = ranks * block_rows

    everyone = gather_relative(latent_cache)
    everyone = everyone.reshape(ranks * slot_count, positions, latent_all)
    slots = jnp.tile(jnp.arange(slot_count, dtype=jnp.int32), ranks)
    request = jnp.arange(ranks * slot_count, dtype=jnp.int32)
    goes_to = destination * slot_count + slots
    source = jnp.sum(
        jnp.where(goes_to[None, :] == request[:, None], request[None, :], 0), axis=1
    )
    moved_len = jnp.sum(
        jnp.where(goes_to[None, :] == request[:, None], lengths[None, :], 0), axis=1
    )
    relative = (source // slot_count) ^ rank_here
    place = (
        ((relative & 1) * chips + ((relative >> 1) & 1) * (chips // 2) + (relative >> 2))
        * slot_count
        + source % slot_count
    )
    moved = everyone[place]
    position_range = jnp.arange(positions, dtype=jnp.int32)

    def inserted(base, fresh, length):
        for step_index in range(step_count):
            writing = position_range[None, :] == (length + step_index)[:, None]
            base = jnp.where(writing[:, :, None], fresh[:, step_index][:, None, :], base)
        return base

    own_first = rank_here * slot_count
    own_len = lax.dynamic_slice_in_dim(moved_len, own_first, slot_count, 0)
    own_cache = inserted(
        lax.dynamic_slice_in_dim(moved, own_first, slot_count, 0), new_latent, own_len
    )
    visible = (
        position_range[None, None, :]
        < (own_len[:, None] + jnp.arange(step_count, dtype=jnp.int32)[None, :] + 1)[:, :, None]
    )
    scores = (
        jnp.einsum("stha,spa->sthp", queries, own_cache, preferred_element_type=jnp.float32)
        * score_scale
    )
    scores = jnp.where(visible[:, :, None, :], scores, -1e30)
    highest = jnp.max(scores, axis=-1, keepdims=True)
    raised = jnp.exp(scores - highest)
    weights = (raised / jnp.sum(raised, axis=-1, keepdims=True)).astype(jnp.bfloat16)

    weight_count = block_rows * heads_here * positions
    fresh_count = block_rows * latent_width
    lane = 128
    sent = jnp.concatenate(
        [
            weights.reshape(weight_count // lane, lane),
            new_latent[..., :latent_width].reshape(fresh_count // lane, lane),
        ]
    )
    arrived = gather_equal(sent, ("chip", "core"), ranks)
    all_weights = arrived[:, : weight_count // lane].reshape(
        ranks * slot_count, step_count, heads_here, positions
    )
    all_fresh = arrived[:, weight_count // lane :].reshape(
        ranks * slot_count, step_count, latent_width
    )
    all_cache = inserted(moved[..., :latent_width], all_fresh, moved_len)
    attended = jnp.einsum(
        "gthp,gpl->gthl", all_weights, all_cache, preferred_element_type=jnp.float32
    ).astype(jnp.bfloat16)
    head_partial = jnp.dot(
        attended.reshape(row_total, heads_here * latent_width),
        w_out.reshape(heads_here * latent_width, column_count),
        preferred_element_type=jnp.float32,
    ).astype(jnp.bfloat16)
    attn_cols = head_partial.astype(jnp.float32)
    for k in range(1, tp_width):
        attn_cols = attn_cols + swap_tp(head_partial, k).astype(jnp.float32)
    mixed = (residual.reshape(row_total, column_count).astype(jnp.float32) + attn_cols).astype(
        jnp.bfloat16
    )

    same_core = gather_equal(mixed, "chip", chips)
    other_core = swap_core(same_core)
    first = jnp.where(core_here == 0, same_core, other_core)
    second = jnp.where(core_here == 0, other_core, same_core)
    rows_in = jnp.stack([first, second], axis=1).transpose(2, 0, 1, 3).reshape(row_total, -1)
    rows_wide = rows_in.astype(jnp.float32)
    inverse_rms = lax.rsqrt(jnp.mean(rows_wide * rows_wide, axis=-1, keepdims=True) + norm_eps)
    normed = (rows_wide * inverse_rms * norm_gain).astype(jnp.bfloat16)
    gate_proj = jnp.dot(normed, w_gate[0], preferred_element_type=jnp.float32)
    up_proj = jnp.dot(normed, w_up[0], preferred_element_type=jnp.float32)
    activated = (jax.nn.silu(gate_proj) * up_proj).astype(jnp.bfloat16)
    expert_terms = jnp.dot(activated, w_down[0], preferred_element_type=jnp.float32)
    top_count = experts.shape[2]
    own_gate = jnp.sum(
        jnp.where(experts == rank_here, gate_weights, 0.0).reshape(row_total, top_count), axis=1
    )
    share = column_count // tp_width
    terms = (
        (expert_terms * own_gate[:, None])
        .astype(jnp.bfloat16)
        .reshape(row_total, chips, 2, tp_width * share)
        .transpose(2, 1, 0, 3)
    )
    mine = lax.dynamic_index_in_dim(terms, core_here, 0, keepdims=False)
    theirs = lax.dynamic_index_in_dim(terms, 1 - core_here, 0, keepdims=False)
    chip_sum = (mine.astype(jnp.float32) + swap_core(theirs).astype(jnp.float32)).astype(
        jnp.bfloat16
    )
    leaving = (
        chip_sum.reshape(chips, row_total, tp_width, share)
        .transpose(0, 2, 1, 3)
        .reshape(chips * tp_width, row_total, share)
    )
    returned = lax.all_to_all(leaving, ("chip", "tp"), 0, 0, tiled=True)
    moe_part = jnp.sum(returned.astype(jnp.float32), axis=0)
    own_columns = lax.dynamic_slice_in_dim(mixed, tp_here * share, share, 1)
    return (
        (own_columns.astype(jnp.float32) + moe_part)
        .astype(jnp.bfloat16)
        .reshape(residual.shape[0], step_count, share)
    )


def solution(mesh):
    groups, ranks, tp_width = (mesh.shape[name] for name in ("groups", "dp", "tp"))
    split = Mesh(
        mesh.devices.reshape(groups, ranks // 2, 2, tp_width), ("groups", "chip", "core", "tp")
    )
    dp = ("chip", "core")
    placed = (
        P(("groups",) + dp, None, None),
        P("groups"),
        P("groups"),
        P(("groups",) + dp, None, "tp", None),
        P(("groups",) + dp, None, None),
        P("groups", None, dp),
        P("tp", None, dp),
        P(),
        P(dp, None, "tp"),
        P(dp, None, "tp"),
        P(dp, "tp", None),
        P("groups", None, None),
        P("groups", None, None),
    )
    return jax.shard_map(
        body,
        mesh=split,
        in_specs=placed,
        out_specs=P("groups", None, dp + ("tp",)),
        check_vma=False,
    )
```

time: 168 us -> 106 us (0.63)
  waiting for transfers between devices: 62.6 us -> 35 us
  blocking collectives: 26.8 us -> 10.6 us
  between operations: 13.7 us -> 0.34 us
  local copies, waits for them, and re-layouts: 31.4 us -> 20.7 us
  starting transfers between devices: 14.5 us -> 19.1 us
  other arithmetic: 4.13 us -> 6.44 us
    all_gather x1 -> x0, waiting for transfers between devices: 30.5 us -> none  [body(): all_attended = lax.all_gather(flat_attended, 'dp', axis=0, tiled=True)]
    ppermute x0 -> x8, waiting for transfers between devices: none -> 16 us  [the longest x4 11 us: swap_chip(): return lax.ppermute(x, 'chip', [(i, i ^ bits) for i in range(count)])]
    all_to_all x3 -> x2, waiting for transfers between devices: 32.1 us -> 19.1 us  [the longest x1 10.2 us: body(): returned = lax.all_to_all(leaving, ('chip', 'tp'), 0, 0, tiled=True)]
    ppermute x0 -> x8, starting transfers between devices: none -> 9.02 us  [the longest x4 7.2 us: swap_chip(): return lax.ppermute(x, 'chip', [(i, i ^ bits) for i in range(count)])]
    psum x1 -> x0, blocking collectives: 8.46 us -> none  [body(): lax.psum(head_partial.astype(jnp.bfloat16), 'tp').astype(jnp.float32)]
    unnamed x20 -> x21, local copies, waits for them, and re-layouts: 9.4 us -> 1.47 us
    all_to_all x1, blocking collectives: 18.3 us -> 10.6 us  [gather_equal(): return lax.all_to_all(spread, axes, 0, 0, tiled=True)]
    all_to_all x3 -> x2, starting transfers between devices: 14.4 us -> 10 us  [the longest x1 5.64 us: gather_equal(): return lax.all_to_all(spread, axes, 0, 0, tiled=True)]
  transfers between devices with their start and end apart: 4 -> 10, of which waited for: 4 -> 7; matrix products, arithmetic and copies ran while one was open for 11% -> 9% of each run, Pallas kernels for 0% -> 0%
where the time goes in v1:
time: 106 us
  waiting for transfers between devices  35 us (33%)
  local copies, waits for them, and re-layouts  20.7 us (20%)
  starting transfers between devices  19.1 us (18%)
  matrix products  13.3 us (13%)
  blocking collectives  10.6 us (10%)
  other arithmetic  6.44 us (6%)
    ppermute x4, waiting for transfers between devices, swap_chip(): return lax.ppermute(x, 'chip', [(i, i ^ bits) for i in range(count)])  11 us
    all_to_all x1, blocking collectives, gather_equal(): return lax.all_to_all(spread, axes, 0, 0, tiled=True)  10.6 us
    all_to_all x1, waiting for transfers between devices, body(): returned = lax.all_to_all(leaving, ('chip', 'tp'), 0, 0, tiled=True)  10.2 us
    all_to_all x1, waiting for transfers between devices, gather_equal(): return lax.all_to_all(spread, axes, 0, 0, tiled=True)  8.91 us
    ppermute x4, starting transfers between devices, swap_chip(): return lax.ppermute(x, 'chip', [(i, i ^ bits) for i in range(count)])  7.2 us
    reshape x1, local copies, waits for them, and re-layouts, body(): w_out.reshape(heads_here * latent_width, column_count)  6.98 us
    all_to_all x1, starting transfers between devices, gather_equal(): return lax.all_to_all(spread, axes, 0, 0, tiled=True)  5.64 us
    dot_general x1, matrix products, body(): jnp.dot(activated, w_down[0], preferred_element_type=jnp.float32)  4.61 us
  transfers between devices with their start and end apart: 10, of which 7 were waited for; matrix products, arithmetic and copies ran while one was open for 9% of the time, Pallas kernels for 0%

profile of v1, /device:TPU:0, one launch (start us, length us, event | category | flops | bytes accessed | tf_op | source)
XLA Modules:
  0.0 105.5 jit_solution(8720126855667380442)
XLA Ops:
  0.0 3.0 %collective-permute-start = (bf16[2,32,576]{2,1,0:T(8,128)(2,1)}, bf16[2,32,576]{2,1,0:T(8,128)(2,1)S(1)}, u32[]{:S(2)}, u32[]{:S(2)}) collective-permute-start(bf16[2,32,576]{2,1,0:T(8,128)(2,1)} %param.13), channel_id=1, source_target_pairs={{0,8},{4,12},{8,0},{12,4},{16,24},{20,28},{24,16},{28,20},{1,9},{5... | collective-permute-start | bytes 221192 | tf_op jit(solution)/shard_map/ppermute | solution.py:16
  3.0 2.6 %collective-permute-start.1 = (bf16[2,32,576]{2,1,0:T(8,128)(2,1)}, bf16[2,32,576]{2,1,0:T(8,128)(2,1)S(1)}, u32[]{:S(2)}, u32[]{:S(2)}) collective-permute-start(bf16[2,32,576]{2,1,0:T(8,128)(2,1)} %param.13), channel_id=1, source_target_pairs={{0,16},{4,20},{8,24},{12,28},{16,0},{20,4},{24,8},{28,12},{1,17},{... | collective-permute-start | bytes 221192 | tf_op jit(solution)/shard_map/ppermute | solution.py:16
  5.7 0.7 multiply_add_fusion
  6.4 0.8 select_reduce_fusion.1
  7.3 5.1 %collective-permute-done.1 = bf16[2,32,576]{2,1,0:T(8,128)(2,1)S(1)} collective-permute-done((bf16[2,32,576]{2,1,0:T(8,128)(2,1)}, bf16[2,32,576]{2,1,0:T(8,128)(2,1)S(1)}, u32[]{:S(2)}, u32[]{:S(2)}) %collective-permute-start.1) | collective-permute-done | bytes 73760 | tf_op jit(solution)/shard_map/ppermute | solution.py:16
  12.5 1.0 fusion.50
  13.4 1.6 %collective-permute-start.3 = (bf16[4,2,32,576]{3,2,1,0:T(8,128)(2,1)S(1)}, bf16[4,2,32,576]{3,2,1,0:T(8,128)(2,1)S(1)}, u32[]{:S(2)}, u32[]{:S(2)}) collective-permute-start(bf16[4,2,32,576]{3,2,1,0:T(8,128)(2,1)S(1)} %get-tuple-element.16), channel_id=1, source_target_pairs={{0,4},{4,0},{8,12},{12,8},{16,20},{20,16},{24,28},{28,24},{1,5},{5... | collective-permute-start | bytes 884744 | tf_op jit(solution)/shard_map/ppermute | solution.py:16
  15.1 5.8 %collective-permute-done.3 = bf16[4,2,32,576]{3,2,1,0:T(8,128)(2,1)S(1)} collective-permute-done((bf16[4,2,32,576]{3,2,1,0:T(8,128)(2,1)S(1)}, bf16[4,2,32,576]{3,2,1,0:T(8,128)(2,1)S(1)}, u32[]{:S(2)}, u32[]{:S(2)}) %collective-permute-start.3) | collective-permute-done | bytes 294944 | tf_op jit(solution)/shard_map/ppermute | solution.py:16
  21.0 0.1 fusion.49
  21.2 7.0 %copy.58 = bf16[32,28,8,512]{3,2,0,1:T(8,128)(2,1)} copy(bf16[32,28,8,512]{3,2,1,0:T(8,128)(2,1)} %bitcast.107) | data formatting | bytes 14680064 | tf_op jit(solution)/shard_map/reshape | solution.py:130
  28.3 1.3 %pad_maximum_fusion = bf16[2,2,4,2,32,576]{5,4,3,2,1,0:T(8,128)(2,1)} fusion(bf16[1,2,4,2,32,576]{5,4,3,2,1,0:T(8,128)(2,1)S(1)} %bitcast.110, bf16[1,2,4,2,32,576]{5,4,3,2,1,0:T(8,128)(2,1)S(1)} %get-tuple-element.9), kind=kLoop, calls=%fused_computation.12 | loop fusion | flops 589824 | bytes 2359296 | tf_op jit(solution)/shard_map/stack | solution.py:28
  29.6 3.3 %gather_fusion = bf16[32,32,576]{2,1,0:T(8,128)(2,1)} fusion(bf16[32,32,576]{2,1,0:T(8,128)(2,1)} %bitcast.108, s32[1024]{0:T(1024)S(1)} %pad_clamp_fusion), kind=kCustom, calls=%fused_computation | custom fusion | bytes 2359424 | tf_op jit(solution)/shard_map/gather | solution.py:81
  32.9 1.2 %fusion.54 = (f32[2,2,32]{2,1,0:T(2,128)S(1)}, f32[2,2,32,32]{2,3,1,0:T(8,128)S(1)}) fusion(bf16[2,2,32,576]{3,2,1,0:T(8,128)(2,1)S(1)} %copy-done, bf16[32,32,576]{2,1,0:T(8,128)(2,1)} %gather_fusion, s32[]{:T(128)S(6)} %select_n.92, pred[2,32]{1,0:T(4,128)(4,1)S(1)} %get-tuple-element.25, pred[2,32]{1,0:T(4,128)(4,1)S(1)} %get-tuple-element.26, ...), kind=kOutput, calls=%fused_computation.97 | convolution fusion | flops 4808735 | bytes 251140 | tf_op jit(solution)/shard_map/sub | solution.py:105
  34.1 0.1 copy.41
  34.2 0.1 reshape.297
  34.3 0.7 broadcast_in_dim.150
  35.0 5.6 %all-to-all-start = ((bf16[16,48,128]{2,1,0:T(8,128)(2,1)}), bf16[16,48,128]{2,1,0:T(8,128)(2,1)S(1)}, u32[]{:S(2)}, u32[]{:S(2)}) async-start(bf16[16,48,128]{2,1,0:T(8,128)(2,1)} %broadcast_in_dim.150), calls=%async_computation | async-start | bytes 393216 | tf_op jit(solution)/shard_map/all_to_all | solution.py:33
  40.8 8.9 %all-to-all-done = bf16[16,48,128]{2,1,0:T(8,128)(2,1)S(1)} async-done(((bf16[16,48,128]{2,1,0:T(8,128)(2,1)}), bf16[16,48,128]{2,1,0:T(8,128)(2,1)S(1)}, u32[]{:S(2)}, u32[]{:S(2)}) %all-to-all-start) | async-done | bytes 196640 | tf_op jit(solution)/shard_map/all_to_all | solution.py:33
  49.7 0.7 slice.42
  50.4 2.0 %reshape.299 = bf16[32,2,32,32]{3,2,1,0:T(8,128)(2,1)} reshape(bf16[16,32,128]{2,1,0:T(8,128)(2,1)} %slice.42) | data formatting | bytes 262144 | tf_op jit(solution)/shard_map/reshape | solution.py:118
  52.4 0.6 slice.43
  53.0 0.9 reshape.300
  53.9 0.1 fusion.52
  54.0 2.3 %convolution_convert_fusion = bf16[32,2,32,512]{3,2,1,0:T(8,128)(2,1)S(1)} fusion(bf16[32,2,32,32]{3,2,1,0:T(8,128)(2,1)} %reshape.299, bf16[32,32,576]{2,1,0:T(8,128)(2,1)} %gather_fusion, pred[32,32]{1,0:T(8,128)(4,1)S(1)} %get-tuple-element.29, pred[32,32]{1,0:T(8,128)(4,1)S(1)} %get-tuple-element.30, bf16[32,512]{1,0:T(8,128)(2,1)S(1)} %bitcast.117, ...), kind=kOutput, calls=%fused_computation.9 | convolution fusion | flops 69206016 | bytes 3737600 | tf_op jit(solution)/shard_map/gthp,gpl->gthl/dot_general | solution.py:125
  56.3 1.2 %copy.59 = bf16[8,8,32,512]{3,1,2,0:T(8,128)(2,1)S(1)} copy(bf16[8,8,32,512]{3,2,1,0:T(8,128)(2,1)S(1)} %bitcast.109) | data formatting | bytes 4194304
  57.6 2.4 %convolution_convert_fusion.1 = bf16[64,224]{1,0:T(8,128)(2,1)S(1)} fusion(bf16[64,16384]{1,0:T(8,128)(2,1)S(1)} %bitcast.106, bf16[16384,224]{0,1:T(8,128)(2,1)S(1)} %bitcast.105), kind=kOutput, calls=%fused_computation.20 | convolution fusion | flops 469776384 | bytes 9465856 | tf_op jit(solution)/shard_map/dot_general | solution.py:128
  60.0 1.5 %collective-permute-start.5 = (bf16[64,224]{1,0:T(8,128)(2,1)S(1)}, bf16[64,224]{1,0:T(8,128)(2,1)S(1)}, u32[]{:S(2)}, u32[]{:S(2)}) collective-permute-start(bf16[64,224]{1,0:T(8,128)(2,1)S(1)} %convolution_convert_fusion.1), channel_id=1, source_target_pairs={{0,1},{1,0},{2,3},{3,2},{4,5},{5,4},{6,7},{7,6},{8,9},{9,8},{10,11... | collective-permute-start | bytes 86024 | tf_op jit(solution)/shard_map/ppermute | solution.py:21
  61.6 2.4 %collective-permute-done.5 = bf16[64,224]{1,0:T(8,128)(2,1)S(1)} collective-permute-done((bf16[64,224]{1,0:T(8,128)(2,1)S(1)}, bf16[64,224]{1,0:T(8,128)(2,1)S(1)}, u32[]{:S(2)}, u32[]{:S(2)}) %collective-permute-start.5) | collective-permute-done | bytes 28704 | tf_op jit(solution)/shard_map/ppermute | solution.py:21
  64.1 10.6 %all_to_all.15 = bf16[8,64,224]{2,1,0:T(8,128)(2,1)S(1)} all-to-all(bf16[8,64,224]{2,1,0:T(8,128)(2,1)S(1)} %broadcast_in_dim.159), channel_id=1, replica_groups=mesh['groups'=1,'chip'=8,'core'=2,'tp'=2] {'chip'}, dimensions={0} | all-to-all | bytes 458752 | tf_op jit(solution)/shard_map/all_to_all | solution.py:33
  74.9 0.1 mul.123
  75.0 1.2 %collective-permute-done.6 = bf16[8,64,224]{2,1,0:T(8,128)(2,1)S(1)} collective-permute-done((bf16[8,64,224]{2,1,0:T(8,128)(2,1)S(1)}, bf16[8,64,224]{2,1,0:T(8,128)(2,1)S(1)}, u32[]{:S(2)}, u32[]{:S(2)}) %collective-permute-start.6) | collective-permute-done | bytes 229408 | tf_op jit(solution)/shard_map/ppermute | solution.py:11
  76.3 0.2 fusion.17
  76.5 0.2 fusion.27
  76.8 0.5 copy.46
  77.3 0.8 convert_element_type.83
  78.1 2.8 %fusion.5 = f32[64,512]{1,0:T(8,128)S(1)} fusion(bf16[64,3584]{1,0:T(8,128)(2,1)S(1)} %convert_element_type.83, bf16[1,3584,512]{2,1,0:T(8,128)(2,1)} %param.21), kind=kOutput, calls=%fused_computation.7 | convolution fusion | flops 234881024 | bytes 4259840 | tf_op jit(solution)/shard_map/dot_general | solution.py:148
  80.8 4.6 %fusion.1 = bf16[64,3584]{1,0:T(8,128)(2,1)S(1)} fusion(bf16[1,512,3584]{2,1,0:T(8,128)(2,1)} %param.23, bf16[64,3584]{1,0:T(8,128)(2,1)S(1)} %convert_element_type.83, bf16[1,3584,512]{2,1,0:T(8,128)(2,1)} %param.22, f32[64]{0:T(128)S(1)} %mul.123, f32[64,512]{1,0:T(8,128)S(1)} %fusion.5), kind=kOutput, calls=%fused_computation.3 | convolution fusion | flops 470417408 | bytes 8388864 | tf_op jit(solution)/shard_map/dot_general | solution.py:151
  85.5 0.8 reshape.303
  86.3 1.1 %constant_dynamic-slice_fusion = (bf16[64,8,1,224]{3,2,1,0:T(2,128)(2,1)S(1)}, bf16[64,8,1,224]{3,2,1,0:T(2,128)(2,1)S(1)}) fusion(bf16[64,8,2,224]{3,2,1,0:T(2,128)(2,1)S(1)} %reshape.303, s32[]{:T(128)S(6)} %select_n.107, s32[]{:T(128)S(6)} %select_n.108), kind=kLoop, calls=%fused_computation.81 | loop fusion | bytes 917512 | tf_op jit(solution)/shard_map/jit(dynamic_index_in_dim)/dynamic_slice | solution.py:163
  87.4 0.1 copy.66
  87.5 0.2 collective-permute-start.7
  87.7 1.4 %collective-permute-done.7 = bf16[8,64,224]{2,1,0:T(8,128)(2,1)S(1)} collective-permute-done((bf16[8,64,224]{2,1,0:T(8,128)(2,1)S(1)}, bf16[8,64,224]{2,1,0:T(8,128)(2,1)S(1)}, u32[]{:S(2)}, u32[]{:S(2)}) %collective-permute-start.7) | collective-permute-done | bytes 229408 | tf_op jit(solution)/shard_map/ppermute | solution.py:11
  89.1 0.2 fusion.28
  89.3 0.1 fusion.51
  89.4 0.7 pad_maximum_fusion.4
  90.2 4.4 %all-to-all-start.2 = ((bf16[16,64,112]{2,1,0:T(8,128)(2,1)}), bf16[16,64,112]{2,1,0:T(8,128)(2,1)S(1)}, u32[]{:S(2)}, u32[]{:S(2)}) async-start(bf16[16,64,112]{2,1,0:T(8,128)(2,1)} %bitcast.28), calls=%async_computation.2 | async-start | bytes 524288 | tf_op jit(solution)/shard_map/all_to_all | solution.py:173
  94.6 10.2 %all-to-all-done.2 = bf16[16,64,112]{2,1,0:T(8,128)(2,1)S(1)} async-done(((bf16[16,64,112]{2,1,0:T(8,128)(2,1)}), bf16[16,64,112]{2,1,0:T(8,128)(2,1)S(1)}, u32[]{:S(2)}, u32[]{:S(2)}) %all-to-all-start.2) | async-done | bytes 229408 | tf_op jit(solution)/shard_map/all_to_all | solution.py:173
  104.8 0.7 add_convert_fusion.1
  (52 shorter events, 1.1 us)
Async XLA Ops:
  0.0 32.9 %copy-start = (bf16[2,2,32,576]{3,2,1,0:T(8,128)(2,1)S(1)}, bf16[2,2,32,576]{3,2,1,0:T(8,128)(2,1)}, u32[]{:S(2)}) copy-start(bf16[2,2,32,576]{3,2,1,0:T(8,128)(2,1)} %param.16) | copy-start | bytes 442372
  0.0 21.2 %slice-start.2 = ((bf16[2,2,576]{2,1,0:T(2,128)(2,1)}), bf16[2,2,512]{2,1,0:T(2,128)(2,1)S(1)}, s32[]{:S(2)}) async-start(bf16[2,2,576]{2,1,0:T(2,128)(2,1)} %param.17), calls=%async_computation.5 | async-start | bytes 8192 | tf_op jit(solution)/shard_map/slice | solution.py:114
  0.0 7.3 %collective-permute-start = (bf16[2,32,576]{2,1,0:T(8,128)(2,1)}, bf16[2,32,576]{2,1,0:T(8,128)(2,1)S(1)}, u32[]{:S(2)}, u32[]{:S(2)}) collective-permute-start(bf16[2,32,576]{2,1,0:T(8,128)(2,1)} %param.13), channel_id=1, source_target_pairs={{0,8},{4,12},{8,0},{12,4},{16,24},{20,28},{24,16},{28,20},{1,9},{5... | collective-permute-start | bytes 221192 | tf_op jit(solution)/shard_map/ppermute | solution.py:16
  3.0 9.4 %collective-permute-start.1 = (bf16[2,32,576]{2,1,0:T(8,128)(2,1)}, bf16[2,32,576]{2,1,0:T(8,128)(2,1)S(1)}, u32[]{:S(2)}, u32[]{:S(2)}) collective-permute-start(bf16[2,32,576]{2,1,0:T(8,128)(2,1)} %param.13), channel_id=1, source_target_pairs={{0,16},{4,20},{8,24},{12,28},{16,0},{20,4},{24,8},{28,12},{1,17},{... | collective-permute-start | bytes 221192 | tf_op jit(solution)/shard_map/ppermute | solution.py:16
  5.6 6.8 %collective-permute-start.2 = (bf16[2,32,576]{2,1,0:T(8,128)(2,1)}, bf16[2,32,576]{2,1,0:T(8,128)(2,1)S(1)}, u32[]{:S(2)}, u32[]{:S(2)}) collective-permute-start(bf16[2,32,576]{2,1,0:T(8,128)(2,1)} %param.13), channel_id=1, source_target_pairs={{0,24},{4,28},{8,16},{12,20},{16,8},{20,12},{24,0},{28,4},{1,25},{... | collective-permute-start | bytes 221192 | tf_op jit(solution)/shard_map/ppermute | solution.py:16
  13.4 7.6 %collective-permute-start.3 = (bf16[4,2,32,576]{3,2,1,0:T(8,128)(2,1)S(1)}, bf16[4,2,32,576]{3,2,1,0:T(8,128)(2,1)S(1)}, u32[]{:S(2)}, u32[]{:S(2)}) collective-permute-start(bf16[4,2,32,576]{3,2,1,0:T(8,128)(2,1)S(1)} %get-tuple-element.16), channel_id=1, source_target_pairs={{0,4},{4,0},{8,12},{12,8},{16,20},{20,16},{24,28},{28,24},{1,5},{5... | collective-permute-start | bytes 884744 | tf_op jit(solution)/shard_map/ppermute | solution.py:16
  21.1 7.2 %collective-permute-start.4 = (bf16[2,4,2,32,576]{4,3,2,1,0:T(8,128)(2,1)S(1)}, bf16[2,4,2,32,576]{4,3,2,1,0:T(8,128)(2,1)S(1)}, u32[]{:S(2)}, u32[]{:S(2)}) collective-permute-start(bf16[2,4,2,32,576]{4,3,2,1,0:T(8,128)(2,1)S(1)} %get-tuple-element.10), channel_id=1, source_target_pairs={{0,2},{2,0},{1,3},{3,1},{4,6},{6,4},{5,7},{7,5},{8,10},{10,8},{9,1... | collective-permute-start | bytes 1769480 | tf_op jit(solution)/shard_map/ppermute | solution.py:11
  21.2 7.0 %copy-start.1 = (bf16[2,2,576]{2,1,0:T(2,128)(2,1)S(1)}, bf16[2,2,576]{2,1,0:T(2,128)(2,1)}, u32[]{:S(2)}) copy-start(bf16[2,2,576]{2,1,0:T(2,128)(2,1)} %param.17) | copy-start | bytes 13828
  29.6 28.0 %slice-start = ((s8[7340032]{0:T(1024)(128)(4,1)}), s8[3145728]{0:T(1024)(128)(4,1)S(1)}, s32[]{:S(2)}) async-start(s8[7340032]{0:T(1024)(128)(4,1)} %bitcast.103), calls=%async_computation.3 | async-start | bytes 6291456
  35.0 14.6 %all-to-all-start = ((bf16[16,48,128]{2,1,0:T(8,128)(2,1)}), bf16[16,48,128]{2,1,0:T(8,128)(2,1)S(1)}, u32[]{:S(2)}, u32[]{:S(2)}) async-start(bf16[16,48,128]{2,1,0:T(8,128)(2,1)} %broadcast_in_dim.150), calls=%async_computation | async-start | bytes 393216 | tf_op jit(solution)/shard_map/all_to_all | solution.py:33
  54.0 3.6 %slice-start.1 = ((s8[7340032]{0:T(1024)(128)(4,1)}), s8[4194304]{0:T(1024)(128)(4,1)S(1)}, s32[]{:S(2)}) async-start(s8[7340032]{0:T(1024)(128)(4,1)} %bitcast.103), calls=%async_computation.4 | async-start | bytes 8388608
  57.6 4.0 %copy-start.2 = (bf16[32,2,224]{2,1,0:T(2,128)(2,1)S(1)}, bf16[32,2,224]{2,1,0:T(2,128)(2,1)}, u32[]{:S(2)}) copy-start(bf16[32,2,224]{2,1,0:T(2,128)(2,1)} %param.18) | copy-start | bytes 86020
  57.6 17.1 %copy-start.3 = (f32[3584]{0:T(1024)S(1)}, f32[3584]{0:T(1024)}, u32[]{:S(2)}) copy-start(f32[3584]{0:T(1024)} %param.20) | copy-start | bytes 43012
  57.6 17.2 %copy-start.4 = (f32[32,2,8]{0,2,1:T(8,128)S(1)}, f32[32,2,8]{0,2,1:T(8,128)}, u32[]{:S(2)}) copy-start(f32[32,2,8]{0,2,1:T(8,128)} %param.25) | copy-start | bytes 6148
  57.6 17.2 %copy-start.5 = (s32[32,2,8]{0,2,1:T(8,128)S(1)}, s32[32,2,8]{0,2,1:T(8,128)}, u32[]{:S(2)}) copy-start(s32[32,2,8]{0,2,1:T(8,128)} %param.24) | copy-start | bytes 6148
  60.0 4.0 %collective-permute-start.5 = (bf16[64,224]{1,0:T(8,128)(2,1)S(1)}, bf16[64,224]{1,0:T(8,128)(2,1)S(1)}, u32[]{:S(2)}, u32[]{:S(2)}) collective-permute-start(bf16[64,224]{1,0:T(8,128)(2,1)S(1)} %convolution_convert_fusion.1), channel_id=1, source_target_pairs={{0,1},{1,0},{2,3},{3,2},{4,5},{5,4},{6,7},{7,6},{8,9},{9,8},{10,11... | collective-permute-start | bytes 86024 | tf_op jit(solution)/shard_map/ppermute | solution.py:21
  74.7 1.5 %collective-permute-start.6 = (bf16[8,64,224]{2,1,0:T(8,128)(2,1)S(1)}, bf16[8,64,224]{2,1,0:T(8,128)(2,1)S(1)}, u32[]{:S(2)}, u32[]{:S(2)}) collective-permute-start(bf16[8,64,224]{2,1,0:T(8,128)(2,1)S(1)} %all_to_all.15), channel_id=1, source_target_pairs={{0,2},{2,0},{1,3},{3,1},{4,6},{6,4},{5,7},{7,5},{8,10},{10,8},{9,1... | collective-permute-start | bytes 688136 | tf_op jit(solution)/shard_map/ppermute | solution.py:11
  87.5 1.6 %collective-permute-start.7 = (bf16[8,64,224]{2,1,0:T(8,128)(2,1)S(1)}, bf16[8,64,224]{2,1,0:T(8,128)(2,1)S(1)}, u32[]{:S(2)}, u32[]{:S(2)}) collective-permute-start(bf16[8,64,224]{2,1,0:T(8,128)(2,1)S(1)} %bitcast.112), channel_id=1, source_target_pairs={{0,2},{2,0},{1,3},{3,1},{4,6},{6,4},{5,7},{7,5},{8,10},{10,8},{9,1... | collective-permute-start | bytes 688136 | tf_op jit(solution)/shard_map/ppermute | solution.py:11
  90.2 14.6 %all-to-all-start.2 = ((bf16[16,64,112]{2,1,0:T(8,128)(2,1)}), bf16[16,64,112]{2,1,0:T(8,128)(2,1)S(1)}, u32[]{:S(2)}, u32[]{:S(2)}) async-start(bf16[16,64,112]{2,1,0:T(8,128)(2,1)} %bitcast.28), calls=%async_computation.2 | async-start | bytes 524288 | tf_op jit(solution)/shard_map/all_to_all | solution.py:173

commit v2 on v1

v2 whole, which is shorter than its diff:
```python
import jax
import jax.numpy as jnp
from jax import lax
from jax.experimental import pallas as pl
from jax.experimental.pallas import tpu as pltpu
from jax.sharding import Mesh, PartitionSpec as P

score_scale = 192.0 ** (-0.5)
norm_eps = 1e-06


def swap_core(x):
    return lax.ppermute(x, "core", [(0, 1), (1, 0)])


def swap_chip(x, bits):
    count = lax.axis_size("chip")
    return lax.ppermute(x, "chip", [(i, i ^ bits) for i in range(count)])


def swap_tp(x, bits):
    count = lax.axis_size("tp")
    return lax.ppermute(x, "tp", [(i, i ^ bits) for i in range(count)])


def gather_relative(x):
    chips = lax.axis_size("chip")
    far = [x] + [swap_chip(x, 2 * k) for k in range(1, chips // 2)]
    near = [swap_chip(x, 1)]
    for arrived in far[1:]:
        near.append(swap_chip(arrived, 1))
    return far + near + [swap_core(part) for part in far + near]


def nt_dot(a, b):
    return lax.dot_general(a, b, (((1,), (1,)), ((), ())), preferred_element_type=jnp.float32)


def inserted_rows(base, fresh, length):
    position = lax.broadcasted_iota(jnp.int32, base.shape, 0)
    for step_index, row in enumerate(fresh):
        base = jnp.where(position == length + step_index, row, base)
    return base


def bring_kernel(*refs):
    count = len(refs) // 2
    copies = [
        pltpu.make_async_copy(refs[k], refs[count + k], refs[-1].at[k]) for k in range(count)
    ]
    for copy in copies:
        copy.start()
    for copy in copies:
        copy.wait()


def weigh_kernel(table, *refs):
    parts, (queries, new_latent, out, held, sems) = refs[:-5], refs[-5:]
    slot_count, positions, _ = held.shape
    step_count, heads, _ = queries.shape[1:]
    width = out.shape[1]
    requests = (table.shape[0] - 1) // 2
    rank = table[2 * requests]
    for s in range(slot_count):
        part = table[rank * slot_count + s] // slot_count
        for k, ref in enumerate(parts):

            @pl.when(part == k)
            def _():
                pltpu.make_async_copy(ref.at[s], held.at[s], sems.at[s]).start()

    slabs = []
    for s in range(slot_count):
        length = table[requests + rank * slot_count + s]
        pltpu.make_async_copy(parts[0].at[s], held.at[s], sems.at[s]).wait()
        fresh = [new_latent[s, t : t + 1, :].astype(jnp.float32) for t in range(step_count)]
        keys = inserted_rows(held[s].astype(jnp.float32), fresh, length).astype(jnp.bfloat16)
        rows = queries[s].reshape(step_count * heads, keys.shape[1])
        scores = nt_dot(rows, keys) * score_scale
        step_of = lax.broadcasted_iota(jnp.int32, scores.shape, 0) // heads
        position = lax.broadcasted_iota(jnp.int32, scores.shape, 1)
        scores = jnp.where(position < length + step_of + 1, scores, -1e30)
        raised = jnp.exp(scores - jnp.max(scores, axis=-1, keepdims=True))
        weights = raised / jnp.sum(raised, axis=-1, keepdims=True)
        slabs += [weights[k * 8 : (k + 1) * 8] for k in range(step_count * heads // 8)]
    top = jnp.concatenate(slabs, axis=1)
    row = lax.broadcasted_iota(jnp.int32, (8, width), 0)
    bottom = jnp.zeros((8, width), jnp.float32)
    for s in range(slot_count):
        for t in range(step_count):
            bottom = jnp.where(
                row == s * step_count + t,
                new_latent[s, t : t + 1, :width].astype(jnp.float32),
                bottom,
            )
    out[...] = jnp.concatenate([top, bottom], axis=0).astype(out.dtype)


def project_kernel(table, *refs):
    parts, rest = refs[:-16], refs[-16:]
    sent_same, sent_other, w_out = rest[:3]
    sources, out, targets = rest[3:6], rest[6], rest[7:10]
    caches, wide, keys, attended, sems, load_sems = rest[10:]
    requests, positions, _ = caches.shape
    heads, columns, latent_width = w_out.shape
    chips = sent_same.shape[0]
    slot_count = step_count = 2
    copies = []
    for k, ref in enumerate(parts):
        copies.append(
            pltpu.make_async_copy(
                ref.at[:, :, pl.ds(0, latent_width)],
                caches.at[pl.ds(k * slot_count, slot_count)],
                sems.at[k],
            )
        )
    loads = [
        pltpu.make_async_copy(source, target, load_sems.at[k])
        for k, (source, target) in enumerate(zip(sources, targets))
    ]
    for copy in copies + loads:
        copy.start()
    core = table[2 * requests] % 2
    lanes = 128
    for k, ref in enumerate((sent_same, sent_other)):
        for c in range(chips):
            for g in range(slot_count * step_count):
                wide[k, g, c * 8 : (c + 1) * 8, :] = ref[
                    c, :8, g * lanes : (g + 1) * lanes
                ].astype(jnp.float32)
    per_lane = lanes // positions
    block = chips * positions
    deep = lax.broadcasted_iota(jnp.int32, (lanes, per_lane * block), 0)
    across = lax.broadcasted_iota(jnp.int32, (lanes, per_lane * block), 1)
    spread = (
        (deep // positions == across // block) & (deep % positions == across % positions)
    ).astype(jnp.bfloat16)
    group_rows = 8 * step_count * chips
    row = lax.broadcasted_iota(jnp.int32, (group_rows, per_lane * block), 0)
    lane = lax.broadcasted_iota(jnp.int32, (group_rows, per_lane * block), 1)
    own_block = row % chips == (lane % block) // positions
    for copy in copies:
        copy.wait()
    taken = step_count * chips
    for s in range(slot_count):
        for k in range(2):
            group = s * 2 + k
            for c in range(chips):
                request = (c * 2 + (core ^ k)) * slot_count + s
                length = table[requests + request]
                bottom = (sent_same, sent_other)[k][c, 8:, :].astype(jnp.float32)
                fresh = [
                    bottom[s * step_count + t : s * step_count + t + 1]
                    for t in range(step_count)
                ]
                base = caches[table[request]].astype(jnp.float32)
                keys[c * positions : (c + 1) * positions, :] = inserted_rows(
                    base, fresh, length
                ).astype(jnp.bfloat16)
            rows = [
                wide[k, s * step_count + t, pl.ds(q, chips, stride=8), :]
                for q in range(8)
                for t in range(step_count)
            ]
            packed = jnp.concatenate(rows, axis=0).astype(jnp.bfloat16)
            spaced = jnp.dot(packed, spread, preferred_element_type=jnp.float32)
            spaced = jnp.where(own_block, spaced, 0.0).astype(jnp.bfloat16)
            for r in range(per_lane):
                product = jnp.dot(
                    spaced[:, r * block : (r + 1) * block],
                    keys[...],
                    preferred_element_type=jnp.float32,
                ).astype(jnp.bfloat16)
                for q in range(8):
                    attended[r * 8 + q, group * taken : (group + 1) * taken, :] = product[
                        q * taken : (q + 1) * taken
                    ]
    total = jnp.zeros((attended.shape[1], columns), jnp.float32)
    for h in range(heads):
        total = total + nt_dot(attended[h], w_out[h])
    count = total.shape[0]
    to = lax.broadcasted_iota(jnp.int32, (count, count), 0)
    source = lax.broadcasted_iota(jnp.int32, (count, count), 1)
    core_of, slot_of, step_of = (to // 4) % 2, (to // 2) % 2, to % 2
    relative = jnp.where(core == 0, core_of, 1 - core_of)
    moved = (slot_of * 2 + relative) * taken + step_of * chips + to // 8
    order = (source == moved).astype(jnp.bfloat16)
    out[...] = jnp.dot(
        order, total.astype(jnp.bfloat16), preferred_element_type=jnp.float32
    ).astype(out.dtype)
    for load in loads:
        load.wait()


def expert_kernel(table, same, other, gain, experts, gates, w_gate, w_up, w_down, keep, give):
    chips, rows, columns = same.shape
    features = chips * 2 * columns
    core = table[table.shape[0] - 1] % 2
    squares = jnp.zeros((rows, columns), jnp.float32)
    for ref in (same, other):
        for c in range(chips):
            x = ref[c].astype(jnp.float32)
            squares = squares + x * x
    scale = lax.rsqrt(jnp.sum(squares, axis=1, keepdims=True) / features + norm_eps)
    hidden = w_gate.shape[1]
    gate_proj = jnp.zeros((rows, hidden), jnp.float32)
    up_proj = jnp.zeros((rows, hidden), jnp.float32)
    for k, ref in enumerate((same, other)):
        for c in range(chips):
            block = c * 2 + (core ^ k)
            normed = (ref[c].astype(jnp.float32) * scale * gain[pl.ds(block, 1), :]).astype(
                jnp.bfloat16
            )
            first = pl.multiple_of(block * columns, 32)
            gate_proj += jnp.dot(
                normed, w_gate[pl.ds(first, columns), :], preferred_element_type=jnp.float32
            )
            up_proj += jnp.dot(
                normed, w_up[pl.ds(first, columns), :], preferred_element_type=jnp.float32
            )
    activated = (gate_proj / (1.0 + jnp.exp(-gate_proj)) * up_proj).astype(jnp.bfloat16)
    rank = table[table.shape[0] - 1]
    by_step = jnp.sum(jnp.where(experts[...] == rank, gates[...], 0.0), axis=1)
    steps, requests = by_step.shape
    row = lax.broadcasted_iota(jnp.int32, (rows, requests), 0)
    request = lax.broadcasted_iota(jnp.int32, (rows, requests), 1)
    own_gate = jnp.zeros((rows, 1), jnp.float32)
    for t in range(steps):
        here = request * steps + t == row
        own_gate += jnp.sum(jnp.where(here, by_step[t : t + 1], 0.0), axis=1, keepdims=True)
    share = keep.shape[2]
    tile = 8 * share
    for first in range(0, features, tile):
        terms = own_gate * jnp.dot(
            activated, w_down[:, first : first + tile], preferred_element_type=jnp.float32
        )
        pieces = [terms[:, j * share : (j + 1) * share].astype(keep.dtype) for j in range(8)]

        def put(even, odd):
            for j in range(8):
                target = even if (j // 2) % 2 == 0 else odd
                target[(first // tile) * 4 + (j // 4) * 2 + j % 2] = pieces[j]

        @pl.when(core == 0)
        def _():
            put(keep, give)

        @pl.when(core == 1)
        def _():
            put(give, keep)


VMEM = pl.BlockSpec(memory_space=pltpu.VMEM)
SMEM = pl.BlockSpec(memory_space=pltpu.SMEM)
ANY = pl.BlockSpec(memory_space=pl.ANY)


def in_vmem(x):
    return pltpu.with_memory_space_constraint(x, pltpu.VMEM)


def in_hbm(x):
    return pltpu.with_memory_space_constraint(x, pltpu.HBM)


def bring(*arrays):
    return pl.pallas_call(
        bring_kernel,
        out_shape=[pltpu.VMEM(x.shape, x.dtype) for x in arrays],
        in_specs=[ANY] * len(arrays),
        out_specs=[VMEM] * len(arrays),
        scratch_shapes=[pltpu.SemaphoreType.DMA((len(arrays),))],
        compiler_params=pltpu.CompilerParams(vmem_limit_bytes=2 * 2**20),
        cost_estimate=pl.CostEstimate(
            flops=0, bytes_accessed=sum(2 * x.size * x.dtype.itemsize for x in arrays), transcendentals=0
        ),
        name="bring_to_vmem",
    )(*[in_hbm(x) for x in arrays])


def weigh(table, parts, queries, new_latent, latent_width):
    slot_count, positions, latent_all = parts[0].shape
    return pl.pallas_call(
        weigh_kernel,
        out_shape=jax.ShapeDtypeStruct((16, latent_width), jnp.bfloat16),
        in_specs=[SMEM] + [ANY] * len(parts) + [VMEM] * 2,
        out_specs=VMEM,
        scratch_shapes=[
            pltpu.VMEM((slot_count, positions, latent_all), jnp.bfloat16),
            pltpu.SemaphoreType.DMA((slot_count,)),
        ],
        compiler_params=pltpu.CompilerParams(vmem_limit_bytes=8 * 2**20),
        name="softmax_weights",
    )(table, *parts, in_vmem(queries), in_vmem(new_latent))


def project(table, parts, sent_same, sent_other, w_out, later):
    heads, columns, latent_width = w_out.shape
    slot_count, positions, _ = parts[0].shape
    requests = len(parts) * slot_count
    rows = requests * 2
    return pl.pallas_call(
        project_kernel,
        out_shape=[jax.ShapeDtypeStruct((rows, columns), jnp.bfloat16)]
        + [pltpu.VMEM(x.shape, x.dtype) for x in later],
        in_specs=[SMEM] + [ANY] * len(parts) + [VMEM] * 3 + [ANY] * len(later),
        out_specs=[VMEM] * (1 + len(later)),
        scratch_shapes=[
            pltpu.VMEM((requests, positions, latent_width), jnp.bfloat16),
            pltpu.VMEM((2, 4, sent_same.shape[0] * 8, 128), jnp.float32),
            pltpu.VMEM((sent_same.shape[0] * positions, latent_width), jnp.bfloat16),
            pltpu.VMEM((heads, rows, latent_width), jnp.bfloat16),
            pltpu.SemaphoreType.DMA((len(parts),)),
            pltpu.SemaphoreType.DMA((len(later),)),
        ],
        compiler_params=pltpu.CompilerParams(vmem_limit_bytes=8 * 2**20),
        name="attend_project",
    )(table, *parts, sent_same, sent_other, in_vmem(w_out), *[in_hbm(x) for x in later])


def run_expert(table, same, other, gain, experts, gates, w_gate, w_up, w_down, share):
    chips, rows, _ = same.shape
    shape = jax.ShapeDtypeStruct((chips * 2, rows, share), jnp.bfloat16)
    return pl.pallas_call(
        expert_kernel,
        out_shape=(shape, shape),
        in_specs=[SMEM] + [VMEM] * 8,
        out_specs=(VMEM, VMEM),
        compiler_params=pltpu.CompilerParams(vmem_limit_bytes=8 * 2**20),
        name="expert_mlp",
    )(
        table,
        same,
        other,
        gain,
        experts,
        gates,
        in_vmem(w_gate),
        in_vmem(w_up),
        in_vmem(w_down),
    )


def gather_equal(x, axes, count):
    spread = jnp.broadcast_to(x[None], (count,) + x.shape)
    return lax.all_to_all(spread, axes, 0, 0, tiled=True)


def body(
    latent_cache,
    lengths,
    destination,
    queries,
    new_latent,
    residual,
    w_out,
    norm_gain,
    w_gate,
    w_up,
    w_down,
    experts,
    gate_weights,
):
    chips = lax.axis_size("chip")
    tp_width = lax.axis_size("tp")
    ranks = chips * 2
    chip_here = lax.axis_index("chip")
    core_here = lax.axis_index("core")
    tp_here = lax.axis_index("tp")
    rank_here = chip_here * 2 + core_here
    slot_count, positions, latent_all = latent_cache.shape
    heads_here, latent_width, column_count = w_out.shape
    step_count = queries.shape[1]
    block_rows = slot_count * step_count
    row_total = ranks * block_rows

    with_kernels = (
        slot_count == 2
        and step_count == 2
        and chips == 8
        and tp_width == 2
        and (positions, heads_here, latent_width, column_count) == (32, 32, 512, 224)
    )
    parts = gather_relative(latent_cache)
    slots = jnp.tile(jnp.arange(slot_count, dtype=jnp.int32), ranks)
    request = jnp.arange(ranks * slot_count, dtype=jnp.int32)
    goes_to = destination * slot_count + slots
    source = jnp.sum(
        jnp.where(goes_to[None, :] == request[:, None], request[None, :], 0), axis=1
    )
    moved_len = jnp.sum(
        jnp.where(goes_to[None, :] == request[:, None], lengths[None, :], 0), axis=1
    )
    relative = (source // slot_count) ^ rank_here
    place = (
        ((relative & 1) * chips + ((relative >> 1) & 1) * (chips // 2) + (relative >> 2))
        * slot_count
        + source % slot_count
    )
    own_gate = jnp.sum(jnp.where(experts == rank_here, gate_weights, 0.0), axis=2).reshape(
        row_total, 1
    )
    share = column_count // tp_width
    first_column = tp_here * share
    residual_rows = residual.reshape(row_total, column_count)
    gain_rows = norm_gain.reshape(ranks, column_count)
    if with_kernels:
        table = jnp.concatenate([place, moved_len, rank_here[None]]).astype(jnp.int32)
        w_columns, near_queries, near_fresh, near_cache = bring(
            jnp.swapaxes(w_out, 1, 2), queries, new_latent, latent_cache
        )
        table, residual_rows, gain_rows, first_column, w_columns = lax.optimization_barrier(
            (table, residual_rows, gain_rows, first_column, w_columns)
        )
        sent = weigh(
            table, [near_cache] + parts[1:], near_queries, near_fresh, latent_width
        )
        sent_same = gather_equal(sent, "chip", chips)
        head_partial, *expert_weights = project(
            table,
            [near_cache] + parts[1:],
            sent_same,
            swap_core(sent_same),
            w_columns,
            (w_gate[0], w_up[0], w_down[0]),
        )
    else:
        moved = jnp.concatenate(parts).reshape(ranks * slot_count, positions, latent_all)[place]
        position_range = jnp.arange(positions, dtype=jnp.int32)

        def inserted(base, fresh, length):
            for step_index in range(step_count):
                writing = position_range[None, :] == (length + step_index)[:, None]
                base = jnp.where(writing[:, :, None], fresh[:, step_index][:, None, :], base)
            return base

        own_first = rank_here * slot_count
        own_len = lax.dynamic_slice_in_dim(moved_len, own_first, slot_count, 0)
        own_cache = inserted(
            lax.dynamic_slice_in_dim(moved, own_first, slot_count, 0), new_latent, own_len
        )
        visible = (
            position_range[None, None, :]
            < (own_len[:, None] + jnp.arange(step_count, dtype=jnp.int32)[None, :] + 1)[:, :, None]
        )
        scores = (
            jnp.einsum("stha,spa->sthp", queries, own_cache, preferred_element_type=jnp.float32)
            * score_scale
        )
        scores = jnp.where(visible[:, :, None, :], scores, -1e30)
        highest = jnp.max(scores, axis=-1, keepdims=True)
        raised = jnp.exp(scores - highest)
        weights = (raised / jnp.sum(raised, axis=-1, keepdims=True)).astype(jnp.bfloat16)

        weight_count = block_rows * heads_here * positions
        fresh_count = block_rows * latent_width
        lane = 128
        sent = jnp.concatenate(
            [
                weights.reshape(weight_count // lane, lane),
                new_latent[..., :latent_width].reshape(fresh_count // lane, lane),
            ]
        )
        arrived = gather_equal(sent, ("chip", "core"), ranks)
        all_weights = arrived[:, : weight_count // lane].reshape(
            ranks * slot_count, step_count, heads_here, positions
        )
        all_fresh = arrived[:, weight_count // lane :].reshape(
            ranks * slot_count, step_count, latent_width
        )
        all_cache = inserted(moved[..., :latent_width], all_fresh, moved_len)
        attended = jnp.einsum(
            "gthp,gpl->gthl", all_weights, all_cache, preferred_element_type=jnp.float32
        ).astype(jnp.bfloat16)
        head_partial = jnp.dot(
            attended.reshape(row_total, heads_here * latent_width),
            w_out.reshape(heads_here * latent_width, column_count),
            preferred_element_type=jnp.float32,
        ).astype(jnp.bfloat16)
    attn_cols = head_partial.astype(jnp.float32)
    for k in range(1, tp_width):
        attn_cols = attn_cols + swap_tp(head_partial, k).astype(jnp.float32)
    mixed = (residual_rows.astype(jnp.float32) + attn_cols).astype(
        jnp.bfloat16
    )

    same_core = gather_equal(mixed, "chip", chips)
    other_core = swap_core(same_core)
    if with_kernels:
        mine, theirs = run_expert(
            table,
            same_core,
            other_core,
            gain_rows,
            jnp.transpose(experts, (1, 2, 0)),
            jnp.transpose(gate_weights, (1, 2, 0)),
            *expert_weights,
            share,
        )
        leaving = (mine.astype(jnp.float32) + swap_core(theirs).astype(jnp.float32)).astype(
            jnp.bfloat16
        )
    else:
        first = jnp.where(core_here == 0, same_core, other_core)
        second = jnp.where(core_here == 0, other_core, same_core)
        rows_in = jnp.stack([first, second], axis=1).transpose(2, 0, 1, 3).reshape(row_total, -1)
        rows_wide = rows_in.astype(jnp.float32)
        inverse_rms = lax.rsqrt(jnp.mean(rows_wide * rows_wide, axis=-1, keepdims=True) + norm_eps)
        normed = (rows_wide * inverse_rms * norm_gain).astype(jnp.bfloat16)
        gate_proj = jnp.dot(normed, w_gate[0], preferred_element_type=jnp.float32)
        up_proj = jnp.dot(normed, w_up[0], preferred_element_type=jnp.float32)
        activated = (jax.nn.silu(gate_proj) * up_proj).astype(jnp.bfloat16)
        expert_terms = jnp.dot(activated, w_down[0], preferred_element_type=jnp.float32)
        terms = (
            (expert_terms * own_gate)
            .astype(jnp.bfloat16)
            .reshape(row_total, chips, 2, tp_width * share)
            .transpose(2, 1, 0, 3)
        )
        mine = lax.dynamic_index_in_dim(terms, core_here, 0, keepdims=False)
        theirs = lax.dynamic_index_in_dim(terms, 1 - core_here, 0, keepdims=False)
        chip_sum = (mine.astype(jnp.float32) + swap_core(theirs).astype(jnp.float32)).astype(
            jnp.bfloat16
        )
        leaving = (
            chip_sum.reshape(chips, row_total, tp_width, share)
            .transpose(0, 2, 1, 3)
            .reshape(chips * tp_width, row_total, share)
        )
    returned = lax.all_to_all(leaving, ("chip", "tp"), 0, 0, tiled=True)
    moe_part = jnp.sum(returned.astype(jnp.float32), axis=0)
    own_columns = lax.dynamic_slice_in_dim(mixed, first_column, share, 1)
    return (
        (own_columns.astype(jnp.float32) + moe_part)
        .astype(jnp.bfloat16)
        .reshape(residual.shape[0], step_count, share)
    )


def solution(mesh):
    groups, ranks, tp_width = (mesh.shape[name] for name in ("groups", "dp", "tp"))
    split = Mesh(
        mesh.devices.reshape(groups, ranks // 2, 2, tp_width), ("groups", "chip", "core", "tp")
    )
    dp = ("chip", "core")
    placed = (
        P(("groups",) + dp, None, None),
        P("groups"),
        P("groups"),
        P(("groups",) + dp, None, "tp", None),
        P(("groups",) + dp, None, None),
        P("groups", None, dp),
        P("tp", None, dp),
        P(),
        P(dp, None, "tp"),
        P(dp, None, "tp"),
        P(dp, "tp", None),
        P("groups", None, None),
        P("groups", None, None),
    )
    return jax.shard_map(
        body,
        mesh=split,
        in_specs=placed,
        out_specs=P("groups", None, dp + ("tp",)),
        check_vma=False,
    )
```

time: 106 us -> 80.5 us (0.76)
  local copies, waits for them, and re-layouts: 20.7 us -> 1.71 us
  waiting for transfers between devices: 35 us -> 20.9 us
  Pallas kernels: 0 us -> 13.6 us
  matrix products: 13.3 us -> 0 us
  blocking collectives: 10.6 us -> 22 us
  other arithmetic: 6.44 us -> 3.07 us
    pallas_call x0 -> x4, Pallas kernels: none -> 13.6 us  [the longest x1 5.09 us: project(): pl.pallas_call(project_kernel, out_shape=[jax.ShapeDtypeStruct((rows, col...]
    dot_general x4 -> x0, matrix products: 12.1 us -> none  [the longest x1 4.61 us: body(): jnp.dot(activated, w_down[0], preferred_element_type=jnp.float32)]
    all_to_all x1 -> x2, blocking collectives: 10.6 us -> 22 us  [gather_equal(): return lax.all_to_all(spread, axes, 0, 0, tiled=True)]
    reshape x6 -> x2, local copies, waits for them, and re-layouts: 10.8 us -> 1.59 us  [the longest x1 0.8 us: body(): residual_rows = residual.reshape(row_total, column_count)]
    all_to_all x1 -> x0, waiting for transfers between devices: 8.91 us -> none  [gather_equal(): return lax.all_to_all(spread, axes, 0, 0, tiled=True)]
    ppermute x4 -> x7, waiting for transfers between devices: 11 us -> 2.95 us  [swap_chip(): return lax.ppermute(x, 'chip', [(i, i ^ bits) for i in range(count)])]
    all_to_all x1 -> x0, starting transfers between devices: 5.64 us -> none  [gather_equal(): return lax.all_to_all(spread, axes, 0, 0, tiled=True)]
    ppermute x4 -> x7, starting transfers between devices: 7.2 us -> 11 us  [swap_chip(): return lax.ppermute(x, 'chip', [(i, i ^ bits) for i in range(count)])]
  transfers between devices with their start and end apart: 10 -> 20, of which waited for: 7 -> 11; matrix products, arithmetic and copies ran while one was open for 9% -> 4% of each run, Pallas kernels for 0% -> 4%
where the time goes in v2:
time: 80.5 us; the launch traced here: 80.1 us
  blocking collectives  22 us (27%)
  waiting for transfers between devices  20.9 us (26%)
  starting transfers between devices  18.6 us (23%)
  Pallas kernels  13.6 us (17%)
  other arithmetic  3.07 us (4%)
  local copies, waits for them, and re-layouts  1.71 us (2%)
    all_to_all x2, blocking collectives, gather_equal(): return lax.all_to_all(spread, axes, 0, 0, tiled=True)  22 us
    ppermute x7, starting transfers between devices, swap_chip(): return lax.ppermute(x, 'chip', [(i, i ^ bits) for i in range(count)])  11 us
    all_to_all x1, waiting for transfers between devices, body(): returned = lax.all_to_all(leaving, ('chip', 'tp'), 0, 0, tiled=True)  10.2 us
    ppermute x11, waiting for transfers between devices, swap_core(): return lax.ppermute(x, 'core', [(0, 1), (1, 0)])  5.4 us
    pallas_call x1, Pallas kernels, project(): pl.pallas_call(project_kernel, out_shape=[jax.ShapeDtypeStruct((rows, col...  5.09 us
    all_to_all x1, starting transfers between devices, body(): returned = lax.all_to_all(leaving, ('chip', 'tp'), 0, 0, tiled=True)  4.46 us
    pallas_call x1, Pallas kernels, run_expert(): pl.pallas_call(expert_kernel, out_shape=(shape, shape), in_specs=[SMEM] +...  3.82 us
    pallas_call x1, Pallas kernels, bring(): pl.pallas_call(bring_kernel, out_shape=[pltpu.VMEM(x.shape, x.dtype) for...  3.13 us
  transfers between devices with their start and end apart: 20, of which 11 were waited for; matrix products, arithmetic and copies ran while one was open for 4% of the time, Pallas kernels for 4%

profile of v2, /device:TPU:0, one launch (start us, length us, event | category | flops | bytes accessed | tf_op | source)
XLA Modules:
  0.0 80.1 jit_solution(6751222967730289370)
XLA Ops:
  0.0 5.0 %collective-permute-start.2 = (bf16[2,32,576]{2,1,0:T(8,128)(2,1)}, bf16[2,32,576]{2,1,0:T(8,128)(2,1)S(1)}, u32[]{:S(2)}, u32[]{:S(2)}) collective-permute-start(bf16[2,32,576]{2,1,0:T(8,128)(2,1)} %refs_3_.1), channel_id=1, source_target_pairs={{0,24},{4,28},{8,16},{12,20},{16,8},{20,12},{24,0},{28,4},{1,25},{... | collective-permute-start | bytes 221192 | tf_op jit(solution)/shard_map/ppermute | solution.py:18
  5.1 0.6 collective-permute-start
  5.6 0.0 collective-permute-start.7
  5.6 1.7 %collective-permute-start.3 = (bf16[2,32,576]{2,1,0:T(8,128)(2,1)}, bf16[2,32,576]{2,1,0:T(8,128)(2,1)S(1)}, u32[]{:S(2)}, u32[]{:S(2)}) collective-permute-start(bf16[2,32,576]{2,1,0:T(8,128)(2,1)} %refs_3_.1), channel_id=1, source_target_pairs={{0,4},{4,0},{8,12},{12,8},{16,20},{20,16},{24,28},{28,24},{1,5},{5... | collective-permute-start | bytes 221192 | tf_op jit(solution)/shard_map/ppermute | solution.py:18
  7.4 0.1 tile.10
  7.5 0.7 multiply_add_fusion
  8.1 0.8 select_reduce_fusion.1
  8.9 0.3 collective-permute-start.10
  9.2 2.9 %collective-permute-done.1.refs_2_ = bf16[2,32,576]{2,1,0:T(8,128)(2,1)S(1)} collective-permute-done((bf16[2,32,576]{2,1,0:T(8,128)(2,1)}, bf16[2,32,576]{2,1,0:T(8,128)(2,1)S(1)}, u32[]{:S(2)}, u32[]{:S(2)}) %collective-permute-start.1) | collective-permute-done | bytes 73760 | tf_op jit(solution)/shard_map/ppermute | solution.py:18
  12.1 1.5 %collective-permute-start.6 = (bf16[2,32,576]{2,1,0:T(8,128)(2,1)S(1)}, bf16[2,32,576]{2,1,0:T(8,128)(2,1)S(1)}, u32[]{:S(2)}, u32[]{:S(2)}) collective-permute-start(bf16[2,32,576]{2,1,0:T(8,128)(2,1)S(1)} %collective-permute-done.2.refs_3_), channel_id=1, source_target_pairs={{0,4},{4,0},{8,12},{12,8},{16,20},{20,16},{24,28},{28,24},{1,5},{5... | collective-permute-start | bytes 221192 | tf_op jit(solution)/shard_map/ppermute | solution.py:18
  13.7 0.6 collective-permute-start.5
  14.2 0.0 collective-permute-done.3.refs_4_
  14.2 1.5 %collective-permute-start.4 = (bf16[2,32,576]{2,1,0:T(8,128)(2,1)S(1)}, bf16[2,32,576]{2,1,0:T(8,128)(2,1)S(1)}, u32[]{:S(2)}, u32[]{:S(2)}) collective-permute-start(bf16[2,32,576]{2,1,0:T(8,128)(2,1)S(1)} %collective-permute-done.refs_1_), channel_id=1, source_target_pairs={{0,4},{4,0},{8,12},{12,8},{16,20},{20,16},{24,28},{28,24},{1,5},{5... | collective-permute-start | bytes 221192 | tf_op jit(solution)/shard_map/ppermute | solution.py:18
  15.8 0.8 reshape.14.gain
  16.6 0.8 reshape.13
  17.4 3.1 %bring_to_vmem.1 = (bf16[32,224,512]{2,1,0:T(8,128)(2,1)S(1)}, bf16[2,2,32,576]{3,2,1,0:T(8,128)(2,1)S(1)}, bf16[2,2,576]{2,1,0:T(2,128)(2,1)S(1)}, bf16[2,32,576]{2,1,0:T(8,128)(2,1)S(1)}) custom-call(bf16[32,224,512]{2,1,0:T(8,128)(2,1)} %bitcast.10, bf16[2,2,32,576]{3,2,1,0:T(8,128)(2,1)} %refs_1_.1, bf16[2,2,576]{2,1,0:T(2,128)(2,1)} %refs_2_.1, ...), custom_call_target="tpu_custom_call" | custom-call | bytes 15131648 | tf_op jit(solution)/shard_map/bring_to_vmem/pallas_call | solution.py:267
  20.5 0.0 collective-permute-done.10.refs_11_
  20.5 0.1 collective-permute-start.8
  20.6 0.0 collective-permute-done.6.refs_7_
  20.6 0.5 collective-permute-start.11
  21.1 0.1 collective-permute-start.14
  21.2 0.0 collective-permute-done.5.refs_6_
  21.2 0.4 collective-permute-start.13
  21.6 0.1 collective-permute-start.12
  21.7 0.1 pad_add_fusion.table
  21.8 0.1 collective-permute-done.8.refs_9_
  21.9 0.2 collective-permute-done.11.refs_12_
  22.0 0.4 collective-permute-done.14.refs_15_
  22.4 0.2 collective-permute-done.13.refs_14_
  22.5 0.4 collective-permute-done.12.refs_13_
  22.9 1.6 %softmax_weights.1 = bf16[16,512]{1,0:T(8,128)(2,1)S(1)} custom-call(s32[65]{0:T(128)S(1)} %pad_add_fusion.table, bf16[2,32,576]{2,1,0:T(8,128)(2,1)S(1)} %get-tuple-element.23.refs_0_, bf16[2,32,576]{2,1,0:T(8,128)(2,1)S(1)} %collective-permute-done.refs_1_, bf16[2,32,576]{2,1,0:T(8,128)(2,1)S(1)} %collective-permute-done.1.refs_2_, ...), custom_call_target="tpu_custom_call" | custom-call | tf_op jit(solution)/shard_map/softmax_weights/pallas_call | solution.py:283
  24.5 11.0 %all_to_all.15.refs_16_ = bf16[8,16,512]{2,1,0:T(8,128)(2,1)S(1)} all-to-all(bf16[8,16,512]{2,1,0:T(8,128)(2,1)S(1)} %broadcast_in_dim.43), channel_id=1, replica_groups=mesh['groups'=1,'chip'=8,'core'=2,'tp'=2] {'chip'}, dimensions={0} | all-to-all | bytes 262144 | tf_op jit(solution)/shard_map/all_to_all | solution.py:346
  35.6 0.0 collective-permute-start.15
  35.6 1.3 %collective-permute-done.15.refs_17_ = bf16[8,16,512]{2,1,0:T(8,128)(2,1)S(1)} collective-permute-done((bf16[8,16,512]{2,1,0:T(8,128)(2,1)S(1)}, bf16[8,16,512]{2,1,0:T(8,128)(2,1)S(1)}, u32[]{:S(2)}, u32[]{:S(2)}) %collective-permute-start.15) | collective-permute-done | bytes 131104 | tf_op jit(solution)/shard_map/ppermute | solution.py:13
  36.9 5.1 %attend_project.1 = (bf16[64,224]{1,0:T(8,128)(2,1)S(1)}, bf16[3584,512]{1,0:T(8,128)(2,1)S(1)}, bf16[3584,512]{1,0:T(8,128)(2,1)S(1)}, bf16[512,3584]{1,0:T(8,128)(2,1)S(1)}) custom-call(s32[65]{0:T(128)S(1)} %pad_add_fusion.table, bf16[2,32,576]{2,1,0:T(8,128)(2,1)S(1)} %get-tuple-element.23.refs_0_, bf16[2,32,576]{2,1,0:T(8,128)(2,1)S(1)} %collective-permute-done.refs_1_, ...), custom_call_target="tpu_custom_call" | custom-call | tf_op jit(solution)/shard_map/attend_project/pallas_call | solution.py:302
  42.0 1.6 %collective-permute-start.16 = (bf16[64,224]{1,0:T(8,128)(2,1)S(1)}, bf16[64,224]{1,0:T(8,128)(2,1)S(1)}, u32[]{:S(2)}, u32[]{:S(2)}) collective-permute-start(bf16[64,224]{1,0:T(8,128)(2,1)S(1)} %get-tuple-element.27), channel_id=1, source_target_pairs={{0,1},{1,0},{2,3},{3,2},{4,5},{5,4},{6,7},{7,6},{8,9},{9,8},{10,11... | collective-permute-start | bytes 86024 | tf_op jit(solution)/shard_map/ppermute | solution.py:23
  43.6 2.4 %collective-permute-done.16 = bf16[64,224]{1,0:T(8,128)(2,1)S(1)} collective-permute-done((bf16[64,224]{1,0:T(8,128)(2,1)S(1)}, bf16[64,224]{1,0:T(8,128)(2,1)S(1)}, u32[]{:S(2)}, u32[]{:S(2)}) %collective-permute-start.16) | collective-permute-done | bytes 28704 | tf_op jit(solution)/shard_map/ppermute | solution.py:23
  46.0 10.9 %all_to_all.16.same = bf16[8,64,224]{2,1,0:T(8,128)(2,1)S(1)} all-to-all(bf16[8,64,224]{2,1,0:T(8,128)(2,1)S(1)} %broadcast_in_dim.44), channel_id=1, replica_groups=mesh['groups'=1,'chip'=8,'core'=2,'tp'=2] {'chip'}, dimensions={0} | all-to-all | bytes 458752 | tf_op jit(solution)/shard_map/all_to_all | solution.py:346
  57.0 0.0 collective-permute-start.17
  57.0 1.5 %collective-permute-done.17.other = bf16[8,64,224]{2,1,0:T(8,128)(2,1)S(1)} collective-permute-done((bf16[8,64,224]{2,1,0:T(8,128)(2,1)S(1)}, bf16[8,64,224]{2,1,0:T(8,128)(2,1)S(1)}, u32[]{:S(2)}, u32[]{:S(2)}) %collective-permute-start.17) | collective-permute-done | bytes 229408 | tf_op jit(solution)/shard_map/ppermute | solution.py:13
  58.5 3.8 %expert_mlp.1 = (bf16[16,64,112]{2,1,0:T(8,128)(2,1)S(1)}, bf16[16,64,112]{2,1,0:T(8,128)(2,1)S(1)}) custom-call(s32[65]{0:T(128)S(1)} %pad_add_fusion.table, bf16[8,64,224]{2,1,0:T(8,128)(2,1)S(1)} %all_to_all.16.same, bf16[8,64,224]{2,1,0:T(8,128)(2,1)S(1)} %collective-permute-done.17.other, f32[16,224]{1,0:T(8,128)S(1)} %reshape.14.gain, ...), custom_call_target="tpu_custom_call" | custom-call | tf_op jit(solution)/shard_map/expert_mlp/pallas_call | solution.py:324
  62.3 0.2 collective-permute-start.18
  62.5 1.4 %collective-permute-done.18 = bf16[16,64,112]{2,1,0:T(8,128)(2,1)S(1)} collective-permute-done((bf16[16,64,112]{2,1,0:T(8,128)(2,1)S(1)}, bf16[16,64,112]{2,1,0:T(8,128)(2,1)S(1)}, u32[]{:S(2)}, u32[]{:S(2)}) %collective-permute-start.18) | collective-permute-done | bytes 229408 | tf_op jit(solution)/shard_map/ppermute | solution.py:13
  63.9 0.8 add_convert_fusion
  64.7 4.5 %all-to-all-start.2 = ((bf16[16,64,112]{2,1,0:T(8,128)(2,1)}), bf16[16,64,112]{2,1,0:T(8,128)(2,1)S(1)}, u32[]{:S(2)}, u32[]{:S(2)}) async-start(bf16[16,64,112]{2,1,0:T(8,128)(2,1)} %add_convert_fusion), calls=%async_computation.2 | async-start | bytes 524288 | tf_op jit(solution)/shard_map/all_to_all | solution.py:530
  69.2 10.2 %all-to-all-done.2 = bf16[16,64,112]{2,1,0:T(8,128)(2,1)S(1)} async-done(((bf16[16,64,112]{2,1,0:T(8,128)(2,1)}), bf16[16,64,112]{2,1,0:T(8,128)(2,1)S(1)}, u32[]{:S(2)}, u32[]{:S(2)}) %all-to-all-start.2) | async-done | bytes 229408 | tf_op jit(solution)/shard_map/all_to_all | solution.py:530
  79.3 0.1 convert_reduce_fusion
  79.4 0.7 add_convert_fusion.2
  (16 shorter events, 0.1 us)
Async XLA Ops:
  0.0 8.9 %collective-permute-start.2 = (bf16[2,32,576]{2,1,0:T(8,128)(2,1)}, bf16[2,32,576]{2,1,0:T(8,128)(2,1)S(1)}, u32[]{:S(2)}, u32[]{:S(2)}) collective-permute-start(bf16[2,32,576]{2,1,0:T(8,128)(2,1)} %refs_3_.1), channel_id=1, source_target_pairs={{0,24},{4,28},{8,16},{12,20},{16,8},{20,12},{24,0},{28,4},{1,25},{... | collective-permute-start | bytes 221192 | tf_op jit(solution)/shard_map/ppermute | solution.py:18
  5.0 7.1 %collective-permute-start.1 = (bf16[2,32,576]{2,1,0:T(8,128)(2,1)}, bf16[2,32,576]{2,1,0:T(8,128)(2,1)S(1)}, u32[]{:S(2)}, u32[]{:S(2)}) collective-permute-start(bf16[2,32,576]{2,1,0:T(8,128)(2,1)} %refs_3_.1), channel_id=1, source_target_pairs={{0,16},{4,20},{8,24},{12,28},{16,0},{20,4},{24,8},{28,12},{1,17},{... | collective-permute-start | bytes 221192 | tf_op jit(solution)/shard_map/ppermute | solution.py:18
  5.1 8.6 %collective-permute-start = (bf16[2,32,576]{2,1,0:T(8,128)(2,1)}, bf16[2,32,576]{2,1,0:T(8,128)(2,1)S(1)}, u32[]{:S(2)}, u32[]{:S(2)}) collective-permute-start(bf16[2,32,576]{2,1,0:T(8,128)(2,1)} %refs_3_.1), channel_id=1, source_target_pairs={{0,8},{4,12},{8,0},{12,4},{16,24},{20,28},{24,16},{28,20},{1,9},{5... | collective-permute-start | bytes 221192 | tf_op jit(solution)/shard_map/ppermute | solution.py:18
  5.6 8.0 %collective-permute-start.7 = (bf16[2,32,576]{2,1,0:T(8,128)(2,1)}, bf16[2,32,576]{2,1,0:T(8,128)(2,1)S(1)}, u32[]{:S(2)}, u32[]{:S(2)}) collective-permute-start(bf16[2,32,576]{2,1,0:T(8,128)(2,1)} %refs_3_.1), channel_id=1, source_target_pairs={{0,2},{2,0},{1,3},{3,1},{4,6},{6,4},{5,7},{7,5},{8,10},{10,8},{9,1... | collective-permute-start | bytes 221192 | tf_op jit(solution)/shard_map/ppermute | solution.py:13
  5.6 8.6 %collective-permute-start.3 = (bf16[2,32,576]{2,1,0:T(8,128)(2,1)}, bf16[2,32,576]{2,1,0:T(8,128)(2,1)S(1)}, u32[]{:S(2)}, u32[]{:S(2)}) collective-permute-start(bf16[2,32,576]{2,1,0:T(8,128)(2,1)} %refs_3_.1), channel_id=1, source_target_pairs={{0,4},{4,0},{8,12},{12,8},{16,20},{20,16},{24,28},{28,24},{1,5},{5... | collective-permute-start | bytes 221192 | tf_op jit(solution)/shard_map/ppermute | solution.py:18
  8.9 11.6 %collective-permute-start.10 = (bf16[2,32,576]{2,1,0:T(8,128)(2,1)S(1)}, bf16[2,32,576]{2,1,0:T(8,128)(2,1)S(1)}, u32[]{:S(2)}, u32[]{:S(2)}) collective-permute-start(bf16[2,32,576]{2,1,0:T(8,128)(2,1)S(1)} %collective-permute-done.2.refs_3_), channel_id=1, source_target_pairs={{0,2},{2,0},{1,3},{3,1},{4,6},{6,4},{5,7},{7,5},{8,10},{10,8},{9,1... | collective-permute-start | bytes 221192 | tf_op jit(solution)/shard_map/ppermute | solution.py:13
  12.1 8.5 %collective-permute-start.6 = (bf16[2,32,576]{2,1,0:T(8,128)(2,1)S(1)}, bf16[2,32,576]{2,1,0:T(8,128)(2,1)S(1)}, u32[]{:S(2)}, u32[]{:S(2)}) collective-permute-start(bf16[2,32,576]{2,1,0:T(8,128)(2,1)S(1)} %collective-permute-done.2.refs_3_), channel_id=1, source_target_pairs={{0,4},{4,0},{8,12},{12,8},{16,20},{20,16},{24,28},{28,24},{1,5},{5... | collective-permute-start | bytes 221192 | tf_op jit(solution)/shard_map/ppermute | solution.py:18
  13.6 7.4 %collective-permute-start.9 = (bf16[2,32,576]{2,1,0:T(8,128)(2,1)S(1)}, bf16[2,32,576]{2,1,0:T(8,128)(2,1)S(1)}, u32[]{:S(2)}, u32[]{:S(2)}) collective-permute-start(bf16[2,32,576]{2,1,0:T(8,128)(2,1)S(1)} %collective-permute-done.1.refs_2_), channel_id=1, source_target_pairs={{0,2},{2,0},{1,3},{3,1},{4,6},{6,4},{5,7},{7,5},{8,10},{10,8},{9,1... | collective-permute-start | bytes 221192 | tf_op jit(solution)/shard_map/ppermute | solution.py:13
  13.7 7.5 %collective-permute-start.5 = (bf16[2,32,576]{2,1,0:T(8,128)(2,1)S(1)}, bf16[2,32,576]{2,1,0:T(8,128)(2,1)S(1)}, u32[]{:S(2)}, u32[]{:S(2)}) collective-permute-start(bf16[2,32,576]{2,1,0:T(8,128)(2,1)S(1)} %collective-permute-done.1.refs_2_), channel_id=1, source_target_pairs={{0,4},{4,0},{8,12},{12,8},{16,20},{20,16},{24,28},{28,24},{1,5},{5... | collective-permute-start | bytes 221192 | tf_op jit(solution)/shard_map/ppermute | solution.py:18
  14.2 7.4 %collective-permute-start.4 = (bf16[2,32,576]{2,1,0:T(8,128)(2,1)S(1)}, bf16[2,32,576]{2,1,0:T(8,128)(2,1)S(1)}, u32[]{:S(2)}, u32[]{:S(2)}) collective-permute-start(bf16[2,32,576]{2,1,0:T(8,128)(2,1)S(1)} %collective-permute-done.refs_1_), channel_id=1, source_target_pairs={{0,4},{4,0},{8,12},{12,8},{16,20},{20,16},{24,28},{28,24},{1,5},{5... | collective-permute-start | bytes 221192 | tf_op jit(solution)/shard_map/ppermute | solution.py:18
  20.5 1.3 %collective-permute-start.8 = (bf16[2,32,576]{2,1,0:T(8,128)(2,1)S(1)}, bf16[2,32,576]{2,1,0:T(8,128)(2,1)S(1)}, u32[]{:S(2)}, u32[]{:S(2)}) collective-permute-start(bf16[2,32,576]{2,1,0:T(8,128)(2,1)S(1)} %collective-permute-done.refs_1_), channel_id=1, source_target_pairs={{0,2},{2,0},{1,3},{3,1},{4,6},{6,4},{5,7},{7,5},{8,10},{10,8},{9,1... | collective-permute-start | bytes 221192 | tf_op jit(solution)/shard_map/ppermute | solution.py:13
  20.6 1.4 %collective-permute-start.11 = (bf16[2,32,576]{2,1,0:T(8,128)(2,1)S(1)}, bf16[2,32,576]{2,1,0:T(8,128)(2,1)S(1)}, u32[]{:S(2)}, u32[]{:S(2)}) collective-permute-start(bf16[2,32,576]{2,1,0:T(8,128)(2,1)S(1)} %collective-permute-done.3.refs_4_), channel_id=1, source_target_pairs={{0,2},{2,0},{1,3},{3,1},{4,6},{6,4},{5,7},{7,5},{8,10},{10,8},{9,1... | collective-permute-start | bytes 221192 | tf_op jit(solution)/shard_map/ppermute | solution.py:13
  21.1 1.3 %collective-permute-start.14 = (bf16[2,32,576]{2,1,0:T(8,128)(2,1)S(1)}, bf16[2,32,576]{2,1,0:T(8,128)(2,1)S(1)}, u32[]{:S(2)}, u32[]{:S(2)}) collective-permute-start(bf16[2,32,576]{2,1,0:T(8,128)(2,1)S(1)} %collective-permute-done.6.refs_7_), channel_id=1, source_target_pairs={{0,2},{2,0},{1,3},{3,1},{4,6},{6,4},{5,7},{7,5},{8,10},{10,8},{9,1... | collective-permute-start | bytes 221192 | tf_op jit(solution)/shard_map/ppermute | solution.py:13
  21.2 1.3 %collective-permute-start.13 = (bf16[2,32,576]{2,1,0:T(8,128)(2,1)S(1)}, bf16[2,32,576]{2,1,0:T(8,128)(2,1)S(1)}, u32[]{:S(2)}, u32[]{:S(2)}) collective-permute-start(bf16[2,32,576]{2,1,0:T(8,128)(2,1)S(1)} %collective-permute-done.5.refs_6_), channel_id=1, source_target_pairs={{0,2},{2,0},{1,3},{3,1},{4,6},{6,4},{5,7},{7,5},{8,10},{10,8},{9,1... | collective-permute-start | bytes 221192 | tf_op jit(solution)/shard_map/ppermute | solution.py:13
  21.6 1.3 %collective-permute-start.12 = (bf16[2,32,576]{2,1,0:T(8,128)(2,1)S(1)}, bf16[2,32,576]{2,1,0:T(8,128)(2,1)S(1)}, u32[]{:S(2)}, u32[]{:S(2)}) collective-permute-start(bf16[2,32,576]{2,1,0:T(8,128)(2,1)S(1)} %collective-permute-done.4.refs_5_), channel_id=1, source_target_pairs={{0,2},{2,0},{1,3},{3,1},{4,6},{6,4},{5,7},{7,5},{8,10},{10,8},{9,1... | collective-permute-start | bytes 221192 | tf_op jit(solution)/shard_map/ppermute | solution.py:13
  35.6 1.3 %collective-permute-start.15 = (bf16[8,16,512]{2,1,0:T(8,128)(2,1)S(1)}, bf16[8,16,512]{2,1,0:T(8,128)(2,1)S(1)}, u32[]{:S(2)}, u32[]{:S(2)}) collective-permute-start(bf16[8,16,512]{2,1,0:T(8,128)(2,1)S(1)} %all_to_all.15.refs_16_), channel_id=1, source_target_pairs={{0,2},{2,0},{1,3},{3,1},{4,6},{6,4},{5,7},{7,5},{8,10},{10,8},{9,1... | collective-permute-start | bytes 393224 | tf_op jit(solution)/shard_map/ppermute | solution.py:13
  36.9 21.6 %copy-start = (s32[32,2,8]{0,2,1:T(8,128)S(1)}, s32[32,2,8]{0,2,1:T(8,128)}, u32[]{:S(2)}) copy-start(s32[32,2,8]{0,2,1:T(8,128)} %param.24) | copy-start | bytes 6148
  36.9 21.6 %copy-start.1 = (f32[32,2,8]{0,2,1:T(8,128)S(1)}, f32[32,2,8]{0,2,1:T(8,128)}, u32[]{:S(2)}) copy-start(f32[32,2,8]{0,2,1:T(8,128)} %param.25) | copy-start | bytes 6148
  42.0 4.0 %collective-permute-start.16 = (bf16[64,224]{1,0:T(8,128)(2,1)S(1)}, bf16[64,224]{1,0:T(8,128)(2,1)S(1)}, u32[]{:S(2)}, u32[]{:S(2)}) collective-permute-start(bf16[64,224]{1,0:T(8,128)(2,1)S(1)} %get-tuple-element.27), channel_id=1, source_target_pairs={{0,1},{1,0},{2,3},{3,2},{4,5},{5,4},{6,7},{7,6},{8,9},{9,8},{10,11... | collective-permute-start | bytes 86024 | tf_op jit(solution)/shard_map/ppermute | solution.py:23
  57.0 1.5 %collective-permute-start.17 = (bf16[8,64,224]{2,1,0:T(8,128)(2,1)S(1)}, bf16[8,64,224]{2,1,0:T(8,128)(2,1)S(1)}, u32[]{:S(2)}, u32[]{:S(2)}) collective-permute-start(bf16[8,64,224]{2,1,0:T(8,128)(2,1)S(1)} %all_to_all.16.same), channel_id=1, source_target_pairs={{0,2},{2,0},{1,3},{3,1},{4,6},{6,4},{5,7},{7,5},{8,10},{10,8},{9,1... | collective-permute-start | bytes 688136 | tf_op jit(solution)/shard_map/ppermute | solution.py:13
  62.3 1.6 %collective-permute-start.18 = (bf16[16,64,112]{2,1,0:T(8,128)(2,1)S(1)}, bf16[16,64,112]{2,1,0:T(8,128)(2,1)S(1)}, u32[]{:S(2)}, u32[]{:S(2)}) collective-permute-start(bf16[16,64,112]{2,1,0:T(8,128)(2,1)S(1)} %get-tuple-element.34), channel_id=1, source_target_pairs={{0,2},{2,0},{1,3},{3,1},{4,6},{6,4},{5,7},{7,5},{8,10},{10,8},{9,1... | collective-permute-start | bytes 688136 | tf_op jit(solution)/shard_map/ppermute | solution.py:13
  64.7 14.6 %all-to-all-start.2 = ((bf16[16,64,112]{2,1,0:T(8,128)(2,1)}), bf16[16,64,112]{2,1,0:T(8,128)(2,1)S(1)}, u32[]{:S(2)}, u32[]{:S(2)}) async-start(bf16[16,64,112]{2,1,0:T(8,128)(2,1)} %add_convert_fusion), calls=%async_computation.2 | async-start | bytes 524288 | tf_op jit(solution)/shard_map/all_to_all | solution.py:530

commit v3 on v2

--- a/solution.py
+++ b/solution.py
@@ -23,13 +23,17 @@
     return lax.ppermute(x, "tp", [(i, i ^ bits) for i in range(count)])
 
 
-def gather_relative(x):
+def gather_relative(x, near_x, table, wanted):
     chips = lax.axis_size("chip")
-    far = [x] + [swap_chip(x, 2 * k) for k in range(1, chips // 2)]
-    near = [swap_chip(x, 1)]
-    for arrived in far[1:]:
-        near.append(swap_chip(arrived, 1))
-    return far + near + [swap_core(part) for part in far + near]
+    far = [swap_chip(x, 2 * k) for k in range(chips // 2 - 1, 0, -1)][::-1]
+    first, table = lax.optimization_barrier((far[0], table))
+    far = [first if part is far[0] else part for part in far]
+    near = [swap_chip(arrived, 1) for arrived in far[::-1]][::-1]
+    if wanted:
+        wanted = lax.optimization_barrier((table, *wanted))[1:]
+        near[2], *wanted = lax.optimization_barrier((near[2], *bring(*wanted)))
+    parts = far[::-1] + [near_x] + near[::-1] + [swap_chip(near_x, 1)]
+    return parts + [swap_core(part) for part in parts], table, wanted
 
 
 def nt_dot(a, b):
@@ -55,26 +59,21 @@
 
 
 def weigh_kernel(table, *refs):
-    parts, (queries, new_latent, out, held, sems) = refs[:-5], refs[-5:]
-    slot_count, positions, _ = held.shape
+    parts, (queries, new_latent, out) = refs[:-3], refs[-3:]
+    slot_count, positions, _ = parts[0].shape
     step_count, heads, _ = queries.shape[1:]
     width = out.shape[1]
-    requests = (table.shape[0] - 1) // 2
-    rank = table[2 * requests]
-    for s in range(slot_count):
-        part = table[rank * slot_count + s] // slot_count
-        for k, ref in enumerate(parts):
-
-            @pl.when(part == k)
-            def _():
-                pltpu.make_async_copy(ref.at[s], held.at[s], sems.at[s]).start()
-
+    requests = len(parts) * slot_count
+    rank = table[table.shape[0] - 2]
     slabs = []
     for s in range(slot_count):
         length = table[requests + rank * slot_count + s]
-        pltpu.make_async_copy(parts[0].at[s], held.at[s], sems.at[s]).wait()
+        place = table[rank * slot_count + s]
+        held = parts[0][s]
+        for k in range(1, len(parts)):
+            held = jnp.where(place == k * slot_count + s, parts[k][s], held)
         fresh = [new_latent[s, t : t + 1, :].astype(jnp.float32) for t in range(step_count)]
-        keys = inserted_rows(held[s].astype(jnp.float32), fresh, length).astype(jnp.bfloat16)
+        keys = inserted_rows(held.astype(jnp.float32), fresh, length).astype(jnp.bfloat16)
         rows = queries[s].reshape(step_count * heads, keys.shape[1])
         scores = nt_dot(rows, keys) * score_scale
         step_of = lax.broadcasted_iota(jnp.int32, scores.shape, 0) // heads
@@ -97,30 +96,24 @@
 
 
 def project_kernel(table, *refs):
-    parts, rest = refs[:-16], refs[-16:]
-    sent_same, sent_other, w_out = rest[:3]
-    sources, out, targets = rest[3:6], rest[6], rest[7:10]
-    caches, wide, keys, attended, sems, load_sems = rest[10:]
-    requests, positions, _ = caches.shape
+    later = refs[-1].shape[0]
+    cut = len(refs) - 11 - 2 * later
+    parts, rest = refs[:cut], refs[cut:]
+    sent_same, sent_other, residual, w_out = rest[:4]
+    sources, (out, residual_rows), targets = rest[4 : 4 + later], rest[4 + later : 6 + later], rest[6 + later : 6 + 2 * later]
+    wide, fresh, keys, attended, load_sems = rest[6 + 2 * later :]
+    slot_count, positions, _ = parts[0].shape
+    requests = len(parts) * slot_count
     heads, columns, latent_width = w_out.shape
     chips = sent_same.shape[0]
-    slot_count = step_count = 2
-    copies = []
-    for k, ref in enumerate(parts):
-        copies.append(
-            pltpu.make_async_copy(
-                ref.at[:, :, pl.ds(0, latent_width)],
-                caches.at[pl.ds(k * slot_count, slot_count)],
-                sems.at[k],
-            )
-        )
+    step_count = 2
     loads = [
         pltpu.make_async_copy(source, target, load_sems.at[k])
         for k, (source, target) in enumerate(zip(sources, targets))
     ]
-    for copy in copies + loads:
-        copy.start()
-    core = table[2 * requests] % 2
+    for load in loads:
+        load.start()
+    core = table[table.shape[0] - 2] % 2
     lanes = 128
     for k, ref in enumerate((sent_same, sent_other)):
         for c in range(chips):
@@ -128,53 +121,64 @@
                 wide[k, g, c * 8 : (c + 1) * 8, :] = ref[
                     c, :8, g * lanes : (g + 1) * lanes
                 ].astype(jnp.float32)
+            fresh[k, c] = ref[c, 8:, :].astype(jnp.float32)
     per_lane = lanes // positions
-    block = chips * positions
-    deep = lax.broadcasted_iota(jnp.int32, (lanes, per_lane * block), 0)
-    across = lax.broadcasted_iota(jnp.int32, (lanes, per_lane * block), 1)
-    spread = (
-        (deep // positions == across // block) & (deep % positions == across % positions)
-    ).astype(jnp.bfloat16)
     group_rows = 8 * step_count * chips
-    row = lax.broadcasted_iota(jnp.int32, (group_rows, per_lane * block), 0)
-    lane = lax.broadcasted_iota(jnp.int32, (group_rows, per_lane * block), 1)
-    own_block = row % chips == (lane % block) // positions
-    for copy in copies:
-        copy.wait()
+    row = lax.broadcasted_iota(jnp.int32, (group_rows, lanes), 0) % chips
+    lane = lax.broadcasted_iota(jnp.int32, (group_rows, lanes), 1) // positions
+    own_block = [row == lane + first for first in range(0, chips, per_lane)]
     taken = step_count * chips
+    spaced = []
     for s in range(slot_count):
         for k in range(2):
-            group = s * 2 + k
-            for c in range(chips):
-                request = (c * 2 + (core ^ k)) * slot_count + s
-                length = table[requests + request]
-                bottom = (sent_same, sent_other)[k][c, 8:, :].astype(jnp.float32)
-                fresh = [
-                    bottom[s * step_count + t : s * step_count + t + 1]
-                    for t in range(step_count)
-                ]
-                base = caches[table[request]].astype(jnp.float32)
-                keys[c * positions : (c + 1) * positions, :] = inserted_rows(
-                    base, fresh, length
-                ).astype(jnp.bfloat16)
             rows = [
                 wide[k, s * step_count + t, pl.ds(q, chips, stride=8), :]
                 for q in range(8)
                 for t in range(step_count)
             ]
-            packed = jnp.concatenate(rows, axis=0).astype(jnp.bfloat16)
-            spaced = jnp.dot(packed, spread, preferred_element_type=jnp.float32)
-            spaced = jnp.where(own_block, spaced, 0.0).astype(jnp.bfloat16)
+            packed = jnp.concatenate(rows, axis=0)
+            turned = []
             for r in range(per_lane):
-                product = jnp.dot(
-                    spaced[:, r * block : (r + 1) * block],
-                    keys[...],
-                    preferred_element_type=jnp.float32,
+                x = jnp.where(lane == r, packed, 0.0)
+                shift = positions
+                while shift < lanes:
+                    x = x + pltpu.roll(x, shift, 1)
+                    shift *= 2
+                turned.append(x)
+            spaced.append(
+                jnp.concatenate(
+                    [
+                        jnp.concatenate([jnp.where(m, x, 0.0) for m in own_block], axis=1)
+                        for x in turned
+                    ],
+                    axis=0,
                 ).astype(jnp.bfloat16)
-                for q in range(8):
-                    attended[r * 8 + q, group * taken : (group + 1) * taken, :] = product[
-                        q * taken : (q + 1) * taken
-                    ]
+            )
+    for n, part in enumerate(parts):
+        for s in range(slot_count):
+            request = table[2 * requests + n * slot_count + s]
+            length = table[requests + request]
+            owner = request // slot_count
+            c = owner // 2
+            k = (owner % 2) ^ core
+            rows = [
+                fresh[k, c, s * step_count + t : s * step_count + t + 1, :]
+                for t in range(step_count)
+            ]
+            first = pl.multiple_of(c * positions, positions)
+            keys[s * 2 + k, pl.ds(first, positions), :] = inserted_rows(
+                part[s, :, :latent_width].astype(jnp.float32), rows, length
+            ).astype(jnp.bfloat16)
+    for s in range(slot_count):
+        for k in range(2):
+            group = s * 2 + k
+            product = jnp.dot(
+                spaced[group], keys[group], preferred_element_type=jnp.float32
+            ).astype(jnp.bfloat16)
+            for h in range(heads):
+                attended[h, group * taken : (group + 1) * taken, :] = product[
+                    h * taken : (h + 1) * taken
+                ]
     total = jnp.zeros((attended.shape[1], columns), jnp.float32)
     for h in range(heads):
         total = total + nt_dot(attended[h], w_out[h])
@@ -188,38 +192,44 @@
     out[...] = jnp.dot(
         order, total.astype(jnp.bfloat16), preferred_element_type=jnp.float32
     ).astype(out.dtype)
+    row = lax.broadcasted_iota(jnp.int32, (count, count // step_count), 0)
+    column = lax.broadcasted_iota(jnp.int32, (count, count // step_count), 1)
+    straight = jnp.zeros((count, columns), jnp.float32)
+    for t in range(step_count):
+        here = (row == column * step_count + t).astype(jnp.bfloat16)
+        straight += jnp.dot(here, residual[:, t, :], preferred_element_type=jnp.float32)
+    residual_rows[...] = straight.astype(residual_rows.dtype)
     for load in loads:
         load.wait()
 
 
-def expert_kernel(table, same, other, gain, experts, gates, w_gate, w_up, w_down, keep, give):
+def expert_kernel(
+    table, same, other, gain, experts, gates, w_gate, w_up, w_down, keep, give, own, normed
+):
     chips, rows, columns = same.shape
     features = chips * 2 * columns
-    core = table[table.shape[0] - 1] % 2
+    rank = table[table.shape[0] - 2]
+    core = rank % 2
     squares = jnp.zeros((rows, columns), jnp.float32)
     for ref in (same, other):
         for c in range(chips):
             x = ref[c].astype(jnp.float32)
             squares = squares + x * x
     scale = lax.rsqrt(jnp.sum(squares, axis=1, keepdims=True) / features + norm_eps)
-    hidden = w_gate.shape[1]
-    gate_proj = jnp.zeros((rows, hidden), jnp.float32)
-    up_proj = jnp.zeros((rows, hidden), jnp.float32)
-    for k, ref in enumerate((same, other)):
-        for c in range(chips):
-            block = c * 2 + (core ^ k)
-            normed = (ref[c].astype(jnp.float32) * scale * gain[pl.ds(block, 1), :]).astype(
-                jnp.bfloat16
-            )
-            first = pl.multiple_of(block * columns, 32)
-            gate_proj += jnp.dot(
-                normed, w_gate[pl.ds(first, columns), :], preferred_element_type=jnp.float32
-            )
-            up_proj += jnp.dot(
-                normed, w_up[pl.ds(first, columns), :], preferred_element_type=jnp.float32
-            )
-    activated = (gate_proj / (1.0 + jnp.exp(-gate_proj)) * up_proj).astype(jnp.bfloat16)
-    rank = table[table.shape[0] - 1]
+    for first in range(0, chips, 2):
+        pieces = []
+        for c in range(first, first + 2):
+            a, b = same[c].astype(jnp.float32), other[c].astype(jnp.float32)
+            pieces.append(jnp.where(core == 0, a, b))
+            pieces.append(jnp.where(core == 0, b, a))
+        width = 4 * columns
+        start = first * 2 * columns
+        gains = [gain[k : k + 1, :] for k in range(start // 128, (start + width) // 128)]
+        normed[:, start : start + width] = (
+            jnp.concatenate(pieces, axis=1) * scale * jnp.concatenate(gains, axis=1)
+        ).astype(normed.dtype)
+    gate_proj = jnp.dot(normed[...], w_gate[...], preferred_element_type=jnp.float32)
+    up_proj = jnp.dot(normed[...], w_up[...], preferred_element_type=jnp.float32)
     by_step = jnp.sum(jnp.where(experts[...] == rank, gates[...], 0.0), axis=1)
     steps, requests = by_step.shape
     row = lax.broadcasted_iota(jnp.int32, (rows, requests), 0)
@@ -228,13 +238,19 @@
     for t in range(steps):
         here = request * steps + t == row
         own_gate += jnp.sum(jnp.where(here, by_step[t : t + 1], 0.0), axis=1, keepdims=True)
+    activated = (gate_proj / (1.0 + jnp.exp(-gate_proj)) * up_proj * own_gate).astype(
+        jnp.bfloat16
+    )
     share = keep.shape[2]
+    mixed = same[rank // 2].astype(jnp.float32)
+    tp = table[table.shape[0] - 1]
+    own[...] = jnp.where(tp == 0, mixed[:, :share], mixed[:, share:]).astype(own.dtype)
     tile = 8 * share
     for first in range(0, features, tile):
-        terms = own_gate * jnp.dot(
+        terms = jnp.dot(
             activated, w_down[:, first : first + tile], preferred_element_type=jnp.float32
-        )
-        pieces = [terms[:, j * share : (j + 1) * share].astype(keep.dtype) for j in range(8)]
+        ).astype(keep.dtype)
+        pieces = [terms[:, j * share : (j + 1) * share] for j in range(8)]
 
         def put(even, odd):
             for j in range(8):
@@ -272,50 +288,55 @@
         scratch_shapes=[pltpu.SemaphoreType.DMA((len(arrays),))],
         compiler_params=pltpu.CompilerParams(vmem_limit_bytes=2 * 2**20),
         cost_estimate=pl.CostEstimate(
-            flops=0, bytes_accessed=sum(2 * x.size * x.dtype.itemsize for x in arrays), transcendentals=0
+            flops=0, bytes_accessed=sum(4 * x.size for x in arrays), transcendentals=0
         ),
         name="bring_to_vmem",
     )(*[in_hbm(x) for x in arrays])
 
 
 def weigh(table, parts, queries, new_latent, latent_width):
-    slot_count, positions, latent_all = parts[0].shape
     return pl.pallas_call(
         weigh_kernel,
         out_shape=jax.ShapeDtypeStruct((16, latent_width), jnp.bfloat16),
-        in_specs=[SMEM] + [ANY] * len(parts) + [VMEM] * 2,
+        in_specs=[SMEM] + [VMEM] * (len(parts) + 2),
         out_specs=VMEM,
-        scratch_shapes=[
-            pltpu.VMEM((slot_count, positions, latent_all), jnp.bfloat16),
-            pltpu.SemaphoreType.DMA((slot_count,)),
-        ],
         compiler_params=pltpu.CompilerParams(vmem_limit_bytes=8 * 2**20),
         name="softmax_weights",
-    )(table, *parts, in_vmem(queries), in_vmem(new_latent))
-
-
-def project(table, parts, sent_same, sent_other, w_out, later):
+    )(table, *[in_vmem(x) for x in (*parts, queries, new_latent)])
+
+
+def project(table, parts, sent_same, sent_other, residual, w_out, later):
     heads, columns, latent_width = w_out.shape
     slot_count, positions, _ = parts[0].shape
-    requests = len(parts) * slot_count
-    rows = requests * 2
+    chips = sent_same.shape[0]
+    rows = residual.shape[0] * residual.shape[1]
+    small = jax.ShapeDtypeStruct((rows, columns), jnp.bfloat16)
     return pl.pallas_call(
         project_kernel,
-        out_shape=[jax.ShapeDtypeStruct((rows, columns), jnp.bfloat16)]
-        + [pltpu.VMEM(x.shape, x.dtype) for x in later],
-        in_specs=[SMEM] + [ANY] * len(parts) + [VMEM] * 3 + [ANY] * len(later),
-        out_specs=[VMEM] * (1 + len(later)),
+        out_shape=[small, small] + [pltpu.VMEM(x.shape, x.dtype) for x in later],
+        in_specs=[SMEM] + [VMEM] * (len(parts) + 4) + [ANY] * len(later),
+        out_specs=[VMEM] * (2 + len(later)),
         scratch_shapes=[
-            pltpu.VMEM((requests, positions, latent_width), jnp.bfloat16),
-            pltpu.VMEM((2, 4, sent_same.shape[0] * 8, 128), jnp.float32),
-            pltpu.VMEM((sent_same.shape[0] * positions, latent_width), jnp.bfloat16),
+            pltpu.VMEM((2, 4, chips * 8, 128), jnp.float32),
+            pltpu.VMEM((2, chips, 8, latent_width), jnp.float32),
+            pltpu.VMEM((4, chips * positions, latent_width), jnp.bfloat16),
             pltpu.VMEM((heads, rows, latent_width), jnp.bfloat16),
-            pltpu.SemaphoreType.DMA((len(parts),)),
             pltpu.SemaphoreType.DMA((len(later),)),
         ],
         compiler_params=pltpu.CompilerParams(vmem_limit_bytes=8 * 2**20),
+        cost_estimate=pl.CostEstimate(
+            flops=0, bytes_accessed=60 * 2**20, transcendentals=0
+        ),
         name="attend_project",
-    )(table, *parts, sent_same, sent_other, in_vmem(w_out), *[in_hbm(x) for x in later])
+    )(
+        table,
+        *[in_vmem(part) for part in parts],
+        sent_same,
+        sent_other,
+        in_vmem(residual),
+        in_vmem(w_out),
+        *[in_hbm(x) for x in later],
+    )
 
 
 def run_expert(table, same, other, gain, experts, gates, w_gate, w_up, w_down, share):
@@ -323,9 +344,12 @@
     shape = jax.ShapeDtypeStruct((chips * 2, rows, share), jnp.bfloat16)
     return pl.pallas_call(
         expert_kernel,
-        out_shape=(shape, shape),
+        out_shape=(shape, shape, jax.ShapeDtypeStruct((rows, share), jnp.bfloat16)),
         in_specs=[SMEM] + [VMEM] * 8,
-        out_specs=(VMEM, VMEM),
+        out_specs=(VMEM, VMEM, VMEM),
+        scratch_shapes=[
+            pltpu.VMEM((rows, gain.size), jnp.bfloat16),
+        ],
         compiler_params=pltpu.CompilerParams(vmem_limit_bytes=8 * 2**20),
         name="expert_mlp",
     )(
@@ -374,6 +398,31 @@
     block_rows = slot_count * step_count
     row_total = ranks * block_rows
 
+    slots = jnp.tile(jnp.arange(slot_count, dtype=jnp.int32), ranks)
+    request = jnp.arange(ranks * slot_count, dtype=jnp.int32)
+    goes_to = destination * slot_count + slots
+    source = jnp.sum(
+        jnp.where(goes_to[None, :] == request[:, None], request[None, :], 0), axis=1
+    )
+    moved_len = jnp.sum(
+        jnp.where(goes_to[None, :] == request[:, None], lengths[None, :], 0), axis=1
+    )
+    relative = (source // slot_count) ^ rank_here
+    place = (
+        (
+            (relative & 1) * chips
+            + ((relative >> 1) & 1) * (chips // 2)
+            + (chips // 2 - 1 - (relative >> 2))
+        )
+        * slot_count
+        + source % slot_count
+    )
+    served = jnp.sum(
+        jnp.where(place[None, :] == request[:, None], request[None, :], 0), axis=1
+    )
+    table = jnp.concatenate(
+        [place, moved_len, served, rank_here[None], tp_here[None]]
+    ).astype(jnp.int32)
     with_kernels = (
         slot_count == 2
         and step_count == 2
@@ -381,48 +430,27 @@
         and tp_width == 2
         and (positions, heads_here, latent_width, column_count) == (32, 32, 512, 224)
     )
-    parts = gather_relative(latent_cache)
-    slots = jnp.tile(jnp.arange(slot_count, dtype=jnp.int32), ranks)
-    request = jnp.arange(ranks * slot_count, dtype=jnp.int32)
-    goes_to = destination * slot_count + slots
-    source = jnp.sum(
-        jnp.where(goes_to[None, :] == request[:, None], request[None, :], 0), axis=1
-    )
-    moved_len = jnp.sum(
-        jnp.where(goes_to[None, :] == request[:, None], lengths[None, :], 0), axis=1
-    )
-    relative = (source // slot_count) ^ rank_here
-    place = (
-        ((relative & 1) * chips + ((relative >> 1) & 1) * (chips // 2) + (relative >> 2))
-        * slot_count
-        + source % slot_count
-    )
+    near_cache = latent_cache
+    if with_kernels:
+        near_cache, near_queries, near_fresh = bring(latent_cache, queries, new_latent)
+    wanted = [jnp.swapaxes(w_out, 1, 2), residual] if with_kernels else []
+    parts, table, wanted = gather_relative(latent_cache, near_cache, table, wanted)
     own_gate = jnp.sum(jnp.where(experts == rank_here, gate_weights, 0.0), axis=2).reshape(
         row_total, 1
     )
     share = column_count // tp_width
-    first_column = tp_here * share
-    residual_rows = residual.reshape(row_total, column_count)
-    gain_rows = norm_gain.reshape(ranks, column_count)
     if with_kernels:
-        table = jnp.concatenate([place, moved_len, rank_here[None]]).astype(jnp.int32)
-        w_columns, near_queries, near_fresh, near_cache = bring(
-            jnp.swapaxes(w_out, 1, 2), queries, new_latent, latent_cache
-        )
-        table, residual_rows, gain_rows, first_column, w_columns = lax.optimization_barrier(
-            (table, residual_rows, gain_rows, first_column, w_columns)
-        )
-        sent = weigh(
-            table, [near_cache] + parts[1:], near_queries, near_fresh, latent_width
-        )
+        w_columns, near_residual = wanted
+        sent = weigh(table, parts, near_queries, near_fresh, latent_width)
         sent_same = gather_equal(sent, "chip", chips)
-        head_partial, *expert_weights = project(
+        head_partial, residual_rows, *expert_weights = project(
             table,
-            [near_cache] + parts[1:],
+            parts,
             sent_same,
             swap_core(sent_same),
+            near_residual,
             w_columns,
-            (w_gate[0], w_up[0], w_down[0]),
+            (w_down[0],),
         )
     else:
         moved = jnp.concatenate(parts).reshape(ranks * slot_count, positions, latent_all)[place]
@@ -477,6 +505,8 @@
             w_out.reshape(heads_here * latent_width, column_count),
             preferred_element_type=jnp.float32,
         ).astype(jnp.bfloat16)
+    if not with_kernels:
+        residual_rows = residual.reshape(row_total, column_count)
     attn_cols = head_partial.astype(jnp.float32)
     for k in range(1, tp_width):
         attn_cols = attn_cols + swap_tp(head_partial, k).astype(jnp.float32)
@@ -487,13 +517,15 @@
     same_core = gather_equal(mixed, "chip", chips)
     other_core = swap_core(same_core)
     if with_kernels:
-        mine, theirs = run_expert(
+        mine, theirs, own_columns = run_expert(
             table,
             same_core,
             other_core,
-            gain_rows,
+            norm_gain.reshape(norm_gain.size // 128, 128),
             jnp.transpose(experts, (1, 2, 0)),
             jnp.transpose(gate_weights, (1, 2, 0)),
+            w_gate[0],
+            w_up[0],
             *expert_weights,
             share,
         )
@@ -529,7 +561,8 @@
         )
     returned = lax.all_to_all(leaving, ("chip", "tp"), 0, 0, tiled=True)
     moe_part = jnp.sum(returned.astype(jnp.float32), axis=0)
-    own_columns = lax.dynamic_slice_in_dim(mixed, first_column, share, 1)
+    if not with_kernels:
+        own_columns = lax.dynamic_slice_in_dim(mixed, tp_here * share, share, 1)
     return (
         (own_columns.astype(jnp.float32) + moe_part)
         .astype(jnp.bfloat16)

time: 80.5 us -> 77.9 us (0.968)
  blocking collectives: 22 us -> 38.2 us
  waiting for transfers between devices: 20.9 us -> 9.58 us
  starting transfers between devices: 18.6 us -> 13.3 us
  local copies, waits for them, and re-layouts: 1.71 us -> 0.22 us
    all_to_all x0 -> x1, blocking collectives: none -> 14.5 us  [body(): returned = lax.all_to_all(leaving, ('chip', 'tp'), 0, 0, tiled=True)]
    all_to_all x1 -> x0, waiting for transfers between devices: 10.2 us -> none  [body(): returned = lax.all_to_all(leaving, ('chip', 'tp'), 0, 0, tiled=True)]
    all_to_all x1 -> x0, starting transfers between devices: 4.46 us -> none  [body(): returned = lax.all_to_all(leaving, ('chip', 'tp'), 0, 0, tiled=True)]
    all_to_all x2, blocking collectives: 22 us -> 23.7 us  [gather_equal(): return lax.all_to_all(spread, axes, 0, 0, tiled=True)]
    reshape x2 -> x0, local copies, waits for them, and re-layouts: 1.59 us -> none  [the longest x1 0.8 us: body(): residual_rows = residual.reshape(row_total, column_count)]
    ppermute x7, starting transfers between devices: 11 us -> 9.8 us  [swap_chip(): return lax.ppermute(x, 'chip', [(i, i ^ bits) for i in range(count)])]
    pallas_call x1 -> x2, Pallas kernels: 3.13 us -> 4.08 us  [bring(): pl.pallas_call(bring_kernel, out_shape=[pltpu.VMEM(x.shape, x.dtype) for...]
    ppermute x7, waiting for transfers between devices: 2.95 us -> 2.07 us  [swap_chip(): return lax.ppermute(x, 'chip', [(i, i ^ bits) for i in range(count)])]
  transfers between devices with their start and end apart: 20 -> 19, of which waited for: 11 -> 10; matrix products, arithmetic and copies ran while one was open for 4% -> 2% of each run, Pallas kernels for 4% -> 5%
where the time goes in v3:
time: 77.9 us; the launch traced here: 77.7 us
  blocking collectives  38.2 us (49%)
  Pallas kernels  13.8 us (18%)
  starting transfers between devices  13.3 us (17%)
  waiting for transfers between devices  9.58 us (12%)
  other arithmetic  2.32 us (3%)
    all_to_all x2, blocking collectives, gather_equal(): return lax.all_to_all(spread, axes, 0, 0, tiled=True)  23.7 us
    all_to_all x1, blocking collectives, body(): returned = lax.all_to_all(leaving, ('chip', 'tp'), 0, 0, tiled=True)  14.5 us
    ppermute x7, starting transfers between devices, swap_chip(): return lax.ppermute(x, 'chip', [(i, i ^ bits) for i in range(count)])  9.8 us
    ppermute x11, waiting for transfers between devices, swap_core(): return lax.ppermute(x, 'core', [(0, 1), (1, 0)])  5.1 us
    pallas_call x1, Pallas kernels, project(): pl.pallas_call(project_kernel, out_shape=[small, small] + [pltpu.VMEM(x.s...  4.99 us
    pallas_call x2, Pallas kernels, bring(): pl.pallas_call(bring_kernel, out_shape=[pltpu.VMEM(x.shape, x.dtype) for...  4.08 us
    pallas_call x1, Pallas kernels, run_expert(): pl.pallas_call(expert_kernel, out_shape=(shape, shape, jax.ShapeDtypeStru...  3.67 us
    ppermute x1, waiting for transfers between devices, swap_tp(): return lax.ppermute(x, 'tp', [(i, i ^ bits) for i in range(count)])  2.42 us
  transfers between devices with their start and end apart: 19, of which 10 were waited for; matrix products, arithmetic and copies ran while one was open for 2% of the time, Pallas kernels for 5%

profile of v3, /device:TPU:0, one launch (start us, length us, event | category | flops | bytes accessed | tf_op | source)
XLA Modules:
  0.0 77.7 jit_solution(6101859888274070157)
XLA Ops:
  0.0 5.0 %collective-permute-start.1 = (bf16[2,32,576]{2,1,0:T(8,128)(2,1)}, bf16[2,32,576]{2,1,0:T(8,128)(2,1)S(1)}, u32[]{:S(2)}, u32[]{:S(2)}) collective-permute-start(bf16[2,32,576]{2,1,0:T(8,128)(2,1)} %refs_0_.1), channel_id=1, source_target_pairs={{0,24},{4,28},{8,16},{12,20},{16,8},{20,12},{24,0},{28,4},{1,25},{... | collective-permute-start | bytes 221192 | tf_op jit(solution)/shard_map/ppermute | solution.py:18
  5.1 0.6 collective-permute-start.2
  5.6 1.0 %bring_to_vmem.2 = (bf16[2,32,576]{2,1,0:T(8,128)(2,1)S(1)}, bf16[2,2,32,576]{3,2,1,0:T(8,128)(2,1)S(1)}, bf16[2,2,576]{2,1,0:T(2,128)(2,1)S(1)}) custom-call(bf16[2,32,576]{2,1,0:T(8,128)(2,1)} %refs_0_.1, bf16[2,2,32,576]{3,2,1,0:T(8,128)(2,1)} %refs_1_.1, bf16[2,2,576]{2,1,0:T(2,128)(2,1)} %refs_2_.1), custom_call_target="tpu_custom_call" | custom-call | bytes 451584 | tf_op jit(solution)/shard_map/bring_to_vmem/pallas_call | solution.py:283
  6.6 0.1 collective-permute-start.10
  6.7 1.8 %collective-permute-start.6 = (bf16[2,32,576]{2,1,0:T(8,128)(2,1)S(1)}, bf16[2,32,576]{2,1,0:T(8,128)(2,1)S(1)}, u32[]{:S(2)}, u32[]{:S(2)}) collective-permute-start(bf16[2,32,576]{2,1,0:T(8,128)(2,1)S(1)} %get-tuple-element.25.refs_3_), channel_id=1, source_target_pairs={{0,4},{4,0},{8,12},{12,8},{16,20},{20,16},{24,28},{28,24},{1,5},{5... | collective-permute-start | bytes 221192 | tf_op jit(solution)/shard_map/ppermute | solution.py:18
  8.5 0.1 tile.10
  8.6 0.7 multiply_add_fusion
  9.3 0.8 select_reduce_fusion.1
  10.0 0.0 collective-permute-done.1.refs_0_
  10.1 0.4 collective-permute-start.3
  10.4 0.1 select_reduce_fusion
  10.5 0.1 concatenate.3.table
  10.6 0.9 %collective-permute-done.refs_2_ = bf16[2,32,576]{2,1,0:T(8,128)(2,1)S(1)} collective-permute-done((bf16[2,32,576]{2,1,0:T(8,128)(2,1)}, bf16[2,32,576]{2,1,0:T(8,128)(2,1)S(1)}, u32[]{:S(2)}, u32[]{:S(2)}) %collective-permute-start) | collective-permute-done | bytes 73760 | tf_op jit(solution)/shard_map/ppermute | solution.py:18
  11.5 1.6 %collective-permute-start.5 = (bf16[2,32,576]{2,1,0:T(8,128)(2,1)S(1)}, bf16[2,32,576]{2,1,0:T(8,128)(2,1)S(1)}, u32[]{:S(2)}, u32[]{:S(2)}) collective-permute-start(bf16[2,32,576]{2,1,0:T(8,128)(2,1)S(1)} %collective-permute-done.refs_2_), channel_id=1, source_target_pairs={{0,4},{4,0},{8,12},{12,8},{16,20},{20,16},{24,28},{28,24},{1,5},{5... | collective-permute-start | bytes 221192 | tf_op jit(solution)/shard_map/ppermute | solution.py:18
  13.1 0.0 collective-permute-done.10.refs_11_
  13.1 0.4 collective-permute-start.4
  13.5 1.2 %collective-permute-done.3.refs_4_ = bf16[2,32,576]{2,1,0:T(8,128)(2,1)S(1)} collective-permute-done((bf16[2,32,576]{2,1,0:T(8,128)(2,1)S(1)}, bf16[2,32,576]{2,1,0:T(8,128)(2,1)S(1)}, u32[]{:S(2)}, u32[]{:S(2)}) %collective-permute-start.3) | collective-permute-done | bytes 73760 | tf_op jit(solution)/shard_map/ppermute | solution.py:18
  14.7 0.0 collective-permute-start.9
  14.7 3.1 %bring_to_vmem.3 = (bf16[32,224,512]{2,1,0:T(8,128)(2,1)S(1)}, bf16[32,2,224]{2,1,0:T(2,128)(2,1)S(1)}) custom-call(bf16[32,224,512]{2,1,0:T(8,128)(2,1)} %bitcast.15, bf16[32,2,224]{2,1,0:T(2,128)(2,1)} %refs_1_.2), custom_call_target="tpu_custom_call" | custom-call | bytes 14737408 | tf_op jit(solution)/shard_map/bring_to_vmem/pallas_call | solution.py:283
  17.8 0.0 collective-permute-done.6.refs_7_
  17.8 0.6 collective-permute-start.8
  18.4 0.1 collective-permute-start.14
  18.5 0.4 collective-permute-start.13
  18.9 0.1 collective-permute-start.12
  19.0 0.4 collective-permute-start.11
  19.4 0.0 collective-permute-done.8.refs_9_
  19.4 0.2 collective-permute-done.14.refs_15_
  19.7 0.2 collective-permute-done.13.refs_14_
  19.8 0.4 collective-permute-done.12.refs_13_
  20.2 0.2 collective-permute-done.11.refs_12_
  20.4 1.1 %softmax_weights.1 = bf16[16,512]{1,0:T(8,128)(2,1)S(1)} custom-call(s32[98]{0:T(128)S(1)} %concatenate.3.table, bf16[2,32,576]{2,1,0:T(8,128)(2,1)S(1)} %collective-permute-done.1.refs_0_, bf16[2,32,576]{2,1,0:T(8,128)(2,1)S(1)} %collective-permute-done.2.refs_1_, bf16[2,32,576]{2,1,0:T(8,128)(2,1)S(1)} %collective-permute-done.refs_2_, ...), custom_call_target="tpu_custom_call" | custom-call | tf_op jit(solution)/shard_map/softmax_weights/pallas_call | solution.py:298
  21.4 12.8 %all_to_all.15.refs_16_ = bf16[8,16,512]{2,1,0:T(8,128)(2,1)S(1)} all-to-all(bf16[8,16,512]{2,1,0:T(8,128)(2,1)S(1)} %broadcast_in_dim.57), channel_id=1, replica_groups=mesh['groups'=1,'chip'=8,'core'=2,'tp'=2] {'chip'}, dimensions={0} | all-to-all | bytes 262144 | tf_op jit(solution)/shard_map/all_to_all | solution.py:370
  34.2 0.0 collective-permute-start.15
  34.2 1.3 %collective-permute-done.15.refs_17_ = bf16[8,16,512]{2,1,0:T(8,128)(2,1)S(1)} collective-permute-done((bf16[8,16,512]{2,1,0:T(8,128)(2,1)S(1)}, bf16[8,16,512]{2,1,0:T(8,128)(2,1)S(1)}, u32[]{:S(2)}, u32[]{:S(2)}) %collective-permute-start.15) | collective-permute-done | bytes 131104 | tf_op jit(solution)/shard_map/ppermute | solution.py:13
  35.6 0.0 copy-start.4
  35.6 5.0 %attend_project.1 = (bf16[64,224]{1,0:T(8,128)(2,1)S(1)}, bf16[64,224]{1,0:T(8,128)(2,1)S(1)}, bf16[512,3584]{1,0:T(8,128)(2,1)S(1)}) custom-call(s32[98]{0:T(128)S(1)} %concatenate.3.table, bf16[2,32,576]{2,1,0:T(8,128)(2,1)S(1)} %collective-permute-done.1.refs_0_, bf16[2,32,576]{2,1,0:T(8,128)(2,1)S(1)} %collective-permute-done.2.refs_1_, ...), custom_call_target="tpu_custom_call" | custom-call | bytes 62914560 | tf_op jit(solution)/shard_map/attend_project/pallas_call | solution.py:314
  40.6 1.6 %collective-permute-start.16 = (bf16[64,224]{1,0:T(8,128)(2,1)S(1)}, bf16[64,224]{1,0:T(8,128)(2,1)S(1)}, u32[]{:S(2)}, u32[]{:S(2)}) collective-permute-start(bf16[64,224]{1,0:T(8,128)(2,1)S(1)} %get-tuple-element.36), channel_id=1, source_target_pairs={{0,1},{1,0},{2,3},{3,2},{4,5},{5,4},{6,7},{7,6},{8,9},{9,8},{10,11... | collective-permute-start | bytes 86024 | tf_op jit(solution)/shard_map/ppermute | solution.py:23
  42.1 2.4 %collective-permute-done.16 = bf16[64,224]{1,0:T(8,128)(2,1)S(1)} collective-permute-done((bf16[64,224]{1,0:T(8,128)(2,1)S(1)}, bf16[64,224]{1,0:T(8,128)(2,1)S(1)}, u32[]{:S(2)}, u32[]{:S(2)}) %collective-permute-start.16) | collective-permute-done | bytes 28704 | tf_op jit(solution)/shard_map/ppermute | solution.py:23
  44.6 10.9 %all_to_all.16.same = bf16[8,64,224]{2,1,0:T(8,128)(2,1)S(1)} all-to-all(bf16[8,64,224]{2,1,0:T(8,128)(2,1)S(1)} %broadcast_in_dim.58), channel_id=1, replica_groups=mesh['groups'=1,'chip'=8,'core'=2,'tp'=2] {'chip'}, dimensions={0} | all-to-all | bytes 458752 | tf_op jit(solution)/shard_map/all_to_all | solution.py:370
  55.5 0.0 collective-permute-start.17
  55.5 1.5 %collective-permute-done.17.other = bf16[8,64,224]{2,1,0:T(8,128)(2,1)S(1)} collective-permute-done((bf16[8,64,224]{2,1,0:T(8,128)(2,1)S(1)}, bf16[8,64,224]{2,1,0:T(8,128)(2,1)S(1)}, u32[]{:S(2)}, u32[]{:S(2)}) %collective-permute-start.17) | collective-permute-done | bytes 229408 | tf_op jit(solution)/shard_map/ppermute | solution.py:13
  57.1 3.7 %expert_mlp.1 = (bf16[16,64,112]{2,1,0:T(8,128)(2,1)S(1)}, bf16[16,64,112]{2,1,0:T(8,128)(2,1)S(1)}, bf16[64,112]{1,0:T(8,128)(2,1)S(1)}) custom-call(s32[98]{0:T(128)S(1)} %concatenate.3.table, bf16[8,64,224]{2,1,0:T(8,128)(2,1)S(1)} %all_to_all.16.same, bf16[8,64,224]{2,1,0:T(8,128)(2,1)S(1)} %collective-permute-done.17.other, f32[28,128]{1,0:T(8,128)S(1)} %bitcast.12, ...), custom_call_target="tpu_custom_call" | custom-call | tf_op jit(solution)/shard_map/expert_mlp/pallas_call | solution.py:345
  60.8 0.3 collective-permute-start.18
  61.1 1.3 %collective-permute-done.18 = bf16[16,64,112]{2,1,0:T(8,128)(2,1)S(1)} collective-permute-done((bf16[16,64,112]{2,1,0:T(8,128)(2,1)S(1)}, bf16[16,64,112]{2,1,0:T(8,128)(2,1)S(1)}, u32[]{:S(2)}, u32[]{:S(2)}) %collective-permute-start.18) | collective-permute-done | bytes 229408 | tf_op jit(solution)/shard_map/ppermute | solution.py:13
  62.4 0.1 add_convert_fusion
  62.4 14.5 %all_to_all.17 = bf16[16,64,112]{2,1,0:T(8,128)(2,1)S(1)} all-to-all(bf16[16,64,112]{2,1,0:T(8,128)(2,1)S(1)} %add_convert_fusion), channel_id=1, replica_groups=mesh['groups'=1,'chip'=8,'core'=2,'tp'=2] {'chip','tp'}, dimensions={0} | all-to-all | bytes 458752 | tf_op jit(solution)/shard_map/all_to_all | solution.py:562
  77.0 0.1 convert_reduce_fusion
  77.0 0.6 add_convert_fusion.2
  (21 shorter events, 0.1 us)
Async XLA Ops:
  0.0 10.0 %collective-permute-start.1 = (bf16[2,32,576]{2,1,0:T(8,128)(2,1)}, bf16[2,32,576]{2,1,0:T(8,128)(2,1)S(1)}, u32[]{:S(2)}, u32[]{:S(2)}) collective-permute-start(bf16[2,32,576]{2,1,0:T(8,128)(2,1)} %refs_0_.1), channel_id=1, source_target_pairs={{0,24},{4,28},{8,16},{12,20},{16,8},{20,12},{24,0},{28,4},{1,25},{... | collective-permute-start | bytes 221192 | tf_op jit(solution)/shard_map/ppermute | solution.py:18
  5.0 6.4 %collective-permute-start = (bf16[2,32,576]{2,1,0:T(8,128)(2,1)}, bf16[2,32,576]{2,1,0:T(8,128)(2,1)S(1)}, u32[]{:S(2)}, u32[]{:S(2)}) collective-permute-start(bf16[2,32,576]{2,1,0:T(8,128)(2,1)} %refs_0_.1), channel_id=1, source_target_pairs={{0,8},{4,12},{8,0},{12,4},{16,24},{20,28},{24,16},{28,20},{1,9},{5... | collective-permute-start | bytes 221192 | tf_op jit(solution)/shard_map/ppermute | solution.py:18
  5.1 6.4 %collective-permute-start.2 = (bf16[2,32,576]{2,1,0:T(8,128)(2,1)}, bf16[2,32,576]{2,1,0:T(8,128)(2,1)S(1)}, u32[]{:S(2)}, u32[]{:S(2)}) collective-permute-start(bf16[2,32,576]{2,1,0:T(8,128)(2,1)} %refs_0_.1), channel_id=1, source_target_pairs={{0,16},{4,20},{8,24},{12,28},{16,0},{20,4},{24,8},{28,12},{1,17},{... | collective-permute-start | bytes 221192 | tf_op jit(solution)/shard_map/ppermute | solution.py:18
  6.6 6.5 %collective-permute-start.10 = (bf16[2,32,576]{2,1,0:T(8,128)(2,1)S(1)}, bf16[2,32,576]{2,1,0:T(8,128)(2,1)S(1)}, u32[]{:S(2)}, u32[]{:S(2)}) collective-permute-start(bf16[2,32,576]{2,1,0:T(8,128)(2,1)S(1)} %get-tuple-element.25.refs_3_), channel_id=1, source_target_pairs={{0,2},{2,0},{1,3},{3,1},{4,6},{6,4},{5,7},{7,5},{8,10},{10,8},{9,1... | collective-permute-start | bytes 221192 | tf_op jit(solution)/shard_map/ppermute | solution.py:13
  6.7 11.1 %collective-permute-start.6 = (bf16[2,32,576]{2,1,0:T(8,128)(2,1)S(1)}, bf16[2,32,576]{2,1,0:T(8,128)(2,1)S(1)}, u32[]{:S(2)}, u32[]{:S(2)}) collective-permute-start(bf16[2,32,576]{2,1,0:T(8,128)(2,1)S(1)} %get-tuple-element.25.refs_3_), channel_id=1, source_target_pairs={{0,4},{4,0},{8,12},{12,8},{16,20},{20,16},{24,28},{28,24},{1,5},{5... | collective-permute-start | bytes 221192 | tf_op jit(solution)/shard_map/ppermute | solution.py:18
  10.1 4.6 %collective-permute-start.3 = (bf16[2,32,576]{2,1,0:T(8,128)(2,1)S(1)}, bf16[2,32,576]{2,1,0:T(8,128)(2,1)S(1)}, u32[]{:S(2)}, u32[]{:S(2)}) collective-permute-start(bf16[2,32,576]{2,1,0:T(8,128)(2,1)S(1)} %collective-permute-done.1.refs_0_), channel_id=1, source_target_pairs={{0,4},{4,0},{8,12},{12,8},{16,20},{20,16},{24,28},{28,24},{1,5},{5... | collective-permute-start | bytes 221192 | tf_op jit(solution)/shard_map/ppermute | solution.py:18
  11.5 6.9 %collective-permute-start.7 = (bf16[2,32,576]{2,1,0:T(8,128)(2,1)S(1)}, bf16[2,32,576]{2,1,0:T(8,128)(2,1)S(1)}, u32[]{:S(2)}, u32[]{:S(2)}) collective-permute-start(bf16[2,32,576]{2,1,0:T(8,128)(2,1)S(1)} %collective-permute-done.1.refs_0_), channel_id=1, source_target_pairs={{0,2},{2,0},{1,3},{3,1},{4,6},{6,4},{5,7},{7,5},{8,10},{10,8},{9,1... | collective-permute-start | bytes 221192 | tf_op jit(solution)/shard_map/ppermute | solution.py:13
  11.5 7.0 %collective-permute-start.5 = (bf16[2,32,576]{2,1,0:T(8,128)(2,1)S(1)}, bf16[2,32,576]{2,1,0:T(8,128)(2,1)S(1)}, u32[]{:S(2)}, u32[]{:S(2)}) collective-permute-start(bf16[2,32,576]{2,1,0:T(8,128)(2,1)S(1)} %collective-permute-done.refs_2_), channel_id=1, source_target_pairs={{0,4},{4,0},{8,12},{12,8},{16,20},{20,16},{24,28},{28,24},{1,5},{5... | collective-permute-start | bytes 221192 | tf_op jit(solution)/shard_map/ppermute | solution.py:18
  13.1 5.8 %collective-permute-start.4 = (bf16[2,32,576]{2,1,0:T(8,128)(2,1)S(1)}, bf16[2,32,576]{2,1,0:T(8,128)(2,1)S(1)}, u32[]{:S(2)}, u32[]{:S(2)}) collective-permute-start(bf16[2,32,576]{2,1,0:T(8,128)(2,1)S(1)} %collective-permute-done.2.refs_1_), channel_id=1, source_target_pairs={{0,4},{4,0},{8,12},{12,8},{16,20},{20,16},{24,28},{28,24},{1,5},{5... | collective-permute-start | bytes 221192 | tf_op jit(solution)/shard_map/ppermute | solution.py:18
  14.7 4.3 %collective-permute-start.9 = (bf16[2,32,576]{2,1,0:T(8,128)(2,1)S(1)}, bf16[2,32,576]{2,1,0:T(8,128)(2,1)S(1)}, u32[]{:S(2)}, u32[]{:S(2)}) collective-permute-start(bf16[2,32,576]{2,1,0:T(8,128)(2,1)S(1)} %collective-permute-done.refs_2_), channel_id=1, source_target_pairs={{0,2},{2,0},{1,3},{3,1},{4,6},{6,4},{5,7},{7,5},{8,10},{10,8},{9,1... | collective-permute-start | bytes 221192 | tf_op jit(solution)/shard_map/ppermute | solution.py:13
  17.8 1.6 %collective-permute-start.8 = (bf16[2,32,576]{2,1,0:T(8,128)(2,1)S(1)}, bf16[2,32,576]{2,1,0:T(8,128)(2,1)S(1)}, u32[]{:S(2)}, u32[]{:S(2)}) collective-permute-start(bf16[2,32,576]{2,1,0:T(8,128)(2,1)S(1)} %collective-permute-done.2.refs_1_), channel_id=1, source_target_pairs={{0,2},{2,0},{1,3},{3,1},{4,6},{6,4},{5,7},{7,5},{8,10},{10,8},{9,1... | collective-permute-start | bytes 221192 | tf_op jit(solution)/shard_map/ppermute | solution.py:13
  18.4 1.3 %collective-permute-start.14 = (bf16[2,32,576]{2,1,0:T(8,128)(2,1)S(1)}, bf16[2,32,576]{2,1,0:T(8,128)(2,1)S(1)}, u32[]{:S(2)}, u32[]{:S(2)}) collective-permute-start(bf16[2,32,576]{2,1,0:T(8,128)(2,1)S(1)} %collective-permute-done.6.refs_7_), channel_id=1, source_target_pairs={{0,2},{2,0},{1,3},{3,1},{4,6},{6,4},{5,7},{7,5},{8,10},{10,8},{9,1... | collective-permute-start | bytes 221192 | tf_op jit(solution)/shard_map/ppermute | solution.py:13
  18.5 1.3 %collective-permute-start.13 = (bf16[2,32,576]{2,1,0:T(8,128)(2,1)S(1)}, bf16[2,32,576]{2,1,0:T(8,128)(2,1)S(1)}, u32[]{:S(2)}, u32[]{:S(2)}) collective-permute-start(bf16[2,32,576]{2,1,0:T(8,128)(2,1)S(1)} %collective-permute-done.5.refs_6_), channel_id=1, source_target_pairs={{0,2},{2,0},{1,3},{3,1},{4,6},{6,4},{5,7},{7,5},{8,10},{10,8},{9,1... | collective-permute-start | bytes 221192 | tf_op jit(solution)/shard_map/ppermute | solution.py:13
  18.9 1.3 %collective-permute-start.12 = (bf16[2,32,576]{2,1,0:T(8,128)(2,1)S(1)}, bf16[2,32,576]{2,1,0:T(8,128)(2,1)S(1)}, u32[]{:S(2)}, u32[]{:S(2)}) collective-permute-start(bf16[2,32,576]{2,1,0:T(8,128)(2,1)S(1)} %collective-permute-done.4.refs_5_), channel_id=1, source_target_pairs={{0,2},{2,0},{1,3},{3,1},{4,6},{6,4},{5,7},{7,5},{8,10},{10,8},{9,1... | collective-permute-start | bytes 221192 | tf_op jit(solution)/shard_map/ppermute | solution.py:13
  19.0 1.3 %collective-permute-start.11 = (bf16[2,32,576]{2,1,0:T(8,128)(2,1)S(1)}, bf16[2,32,576]{2,1,0:T(8,128)(2,1)S(1)}, u32[]{:S(2)}, u32[]{:S(2)}) collective-permute-start(bf16[2,32,576]{2,1,0:T(8,128)(2,1)S(1)} %collective-permute-done.3.refs_4_), channel_id=1, source_target_pairs={{0,2},{2,0},{1,3},{3,1},{4,6},{6,4},{5,7},{7,5},{8,10},{10,8},{9,1... | collective-permute-start | bytes 221192 | tf_op jit(solution)/shard_map/ppermute | solution.py:13
  34.2 1.3 %collective-permute-start.15 = (bf16[8,16,512]{2,1,0:T(8,128)(2,1)S(1)}, bf16[8,16,512]{2,1,0:T(8,128)(2,1)S(1)}, u32[]{:S(2)}, u32[]{:S(2)}) collective-permute-start(bf16[8,16,512]{2,1,0:T(8,128)(2,1)S(1)} %all_to_all.15.refs_16_), channel_id=1, source_target_pairs={{0,2},{2,0},{1,3},{3,1},{4,6},{6,4},{5,7},{7,5},{8,10},{10,8},{9,1... | collective-permute-start | bytes 393224 | tf_op jit(solution)/shard_map/ppermute | solution.py:13
  35.6 21.5 %copy-start = (bf16[1,3584,512]{2,1,0:T(8,128)(2,1)S(1)}, bf16[1,3584,512]{2,1,0:T(8,128)(2,1)}, u32[]{:S(2)}) copy-start(bf16[1,3584,512]{2,1,0:T(8,128)(2,1)} %param.21) | copy-start | bytes 11010052
  35.6 21.5 %copy-start.1 = (bf16[1,3584,512]{2,1,0:T(8,128)(2,1)S(1)}, bf16[1,3584,512]{2,1,0:T(8,128)(2,1)}, u32[]{:S(2)}) copy-start(bf16[1,3584,512]{2,1,0:T(8,128)(2,1)} %param.22) | copy-start | bytes 11010052
  35.6 21.5 %copy-start.2 = (f32[3584]{0:T(1024)S(1)}, f32[3584]{0:T(1024)}, u32[]{:S(2)}) copy-start(f32[3584]{0:T(1024)} %param.20) | copy-start | bytes 43012
  35.6 21.5 %copy-start.3 = (s32[32,2,8]{0,2,1:T(8,128)S(1)}, s32[32,2,8]{0,2,1:T(8,128)}, u32[]{:S(2)}) copy-start(s32[32,2,8]{0,2,1:T(8,128)} %param.24) | copy-start | bytes 6148
  35.6 21.5 %copy-start.4 = (f32[32,2,8]{0,2,1:T(8,128)S(1)}, f32[32,2,8]{0,2,1:T(8,128)}, u32[]{:S(2)}) copy-start(f32[32,2,8]{0,2,1:T(8,128)} %param.25) | copy-start | bytes 6148
  40.6 4.0 %collective-permute-start.16 = (bf16[64,224]{1,0:T(8,128)(2,1)S(1)}, bf16[64,224]{1,0:T(8,128)(2,1)S(1)}, u32[]{:S(2)}, u32[]{:S(2)}) collective-permute-start(bf16[64,224]{1,0:T(8,128)(2,1)S(1)} %get-tuple-element.36), channel_id=1, source_target_pairs={{0,1},{1,0},{2,3},{3,2},{4,5},{5,4},{6,7},{7,6},{8,9},{9,8},{10,11... | collective-permute-start | bytes 86024 | tf_op jit(solution)/shard_map/ppermute | solution.py:23
  55.5 1.5 %collective-permute-start.17 = (bf16[8,64,224]{2,1,0:T(8,128)(2,1)S(1)}, bf16[8,64,224]{2,1,0:T(8,128)(2,1)S(1)}, u32[]{:S(2)}, u32[]{:S(2)}) collective-permute-start(bf16[8,64,224]{2,1,0:T(8,128)(2,1)S(1)} %all_to_all.16.same), channel_id=1, source_target_pairs={{0,2},{2,0},{1,3},{3,1},{4,6},{6,4},{5,7},{7,5},{8,10},{10,8},{9,1... | collective-permute-start | bytes 688136 | tf_op jit(solution)/shard_map/ppermute | solution.py:13
  60.8 1.6 %collective-permute-start.18 = (bf16[16,64,112]{2,1,0:T(8,128)(2,1)S(1)}, bf16[16,64,112]{2,1,0:T(8,128)(2,1)S(1)}, u32[]{:S(2)}, u32[]{:S(2)}) collective-permute-start(bf16[16,64,112]{2,1,0:T(8,128)(2,1)S(1)} %get-tuple-element.40), channel_id=1, source_target_pairs={{0,2},{2,0},{1,3},{3,1},{4,6},{6,4},{5,7},{7,5},{8,10},{10,8},{9,1... | collective-permute-start | bytes 688136 | tf_op jit(solution)/shard_map/ppermute | solution.py:13

commit v4 on v3

--- a/solution.py
+++ b/solution.py
@@ -117,11 +117,10 @@
     lanes = 128
     for k, ref in enumerate((sent_same, sent_other)):
         for c in range(chips):
+            chunk = ref[c].astype(jnp.float32)
             for g in range(slot_count * step_count):
-                wide[k, g, c * 8 : (c + 1) * 8, :] = ref[
-                    c, :8, g * lanes : (g + 1) * lanes
-                ].astype(jnp.float32)
-            fresh[k, c] = ref[c, 8:, :].astype(jnp.float32)
+                wide[k, g, c * 8 : (c + 1) * 8, :] = chunk[:8, g * lanes : (g + 1) * lanes]
+            fresh[k, c] = chunk[8:]
     per_lane = lanes // positions
     group_rows = 8 * step_count * chips
     row = lax.broadcasted_iota(jnp.int32, (group_rows, lanes), 0) % chips
@@ -195,9 +194,11 @@
     row = lax.broadcasted_iota(jnp.int32, (count, count // step_count), 0)
     column = lax.broadcasted_iota(jnp.int32, (count, count // step_count), 1)
     straight = jnp.zeros((count, columns), jnp.float32)
+    wide_residual = residual[...].astype(jnp.float32)
     for t in range(step_count):
         here = (row == column * step_count + t).astype(jnp.bfloat16)
-        straight += jnp.dot(here, residual[:, t, :], preferred_element_type=jnp.float32)
+        rows = wide_residual[:, t, :].astype(jnp.bfloat16)
+        straight += jnp.dot(here, rows, preferred_element_type=jnp.float32)
     residual_rows[...] = straight.astype(residual_rows.dtype)
     for load in loads:
         load.wait()

time: 77.9 us -> 77.9 us (level)
  no operation moved by 1% of the time
where the time goes in v4:
time: 77.9 us; the launch traced here: 77.7 us
  blocking collectives  38.2 us (49%)
  Pallas kernels  13.8 us (18%)
  starting transfers between devices  13.3 us (17%)
  waiting for transfers between devices  9.58 us (12%)
  other arithmetic  2.32 us (3%)
    all_to_all x2, blocking collectives, gather_equal(): return lax.all_to_all(spread, axes, 0, 0, tiled=True)  23.7 us
    all_to_all x1, blocking collectives, body(): returned = lax.all_to_all(leaving, ('chip', 'tp'), 0, 0, tiled=True)  14.5 us
    ppermute x7, starting transfers between devices, swap_chip(): return lax.ppermute(x, 'chip', [(i, i ^ bits) for i in range(count)])  9.8 us
    ppermute x11, waiting for transfers between devices, swap_core(): return lax.ppermute(x, 'core', [(0, 1), (1, 0)])  5.1 us
    pallas_call x1, Pallas kernels, project(): pl.pallas_call(project_kernel, out_shape=[small, small] + [pltpu.VMEM(x.s...  4.99 us
    pallas_call x2, Pallas kernels, bring(): pl.pallas_call(bring_kernel, out_shape=[pltpu.VMEM(x.shape, x.dtype) for...  4.08 us
    pallas_call x1, Pallas kernels, run_expert(): pl.pallas_call(expert_kernel, out_shape=(shape, shape, jax.ShapeDtypeStru...  3.66 us
    ppermute x1, waiting for transfers between devices, swap_tp(): return lax.ppermute(x, 'tp', [(i, i ^ bits) for i in range(count)])  2.42 us
  transfers between devices with their start and end apart: 19, of which 10 were waited for; matrix products, arithmetic and copies ran while one was open for 2% of the time, Pallas kernels for 5%

profile of v4, /device:TPU:0, one launch (start us, length us, event | category | flops | bytes accessed | tf_op | source)
XLA Modules:
  0.0 77.7 jit_solution(3177497836826358636)
XLA Ops:
  0.0 5.0 %collective-permute-start.1 = (bf16[2,32,576]{2,1,0:T(8,128)(2,1)}, bf16[2,32,576]{2,1,0:T(8,128)(2,1)S(1)}, u32[]{:S(2)}, u32[]{:S(2)}) collective-permute-start(bf16[2,32,576]{2,1,0:T(8,128)(2,1)} %refs_0_.1), channel_id=1, source_target_pairs={{0,24},{4,28},{8,16},{12,20},{16,8},{20,12},{24,0},{28,4},{1,25},{... | collective-permute-start | bytes 221192 | tf_op jit(solution)/shard_map/ppermute | solution.py:18
  5.0 0.0 collective-permute-start
  5.1 0.6 collective-permute-start.2
  5.6 1.0 %bring_to_vmem.2 = (bf16[2,32,576]{2,1,0:T(8,128)(2,1)S(1)}, bf16[2,2,32,576]{3,2,1,0:T(8,128)(2,1)S(1)}, bf16[2,2,576]{2,1,0:T(2,128)(2,1)S(1)}) custom-call(bf16[2,32,576]{2,1,0:T(8,128)(2,1)} %refs_0_.1, bf16[2,2,32,576]{3,2,1,0:T(8,128)(2,1)} %refs_1_.1, bf16[2,2,576]{2,1,0:T(2,128)(2,1)} %refs_2_.1), custom_call_target="tpu_custom_call" | custom-call | bytes 451584 | tf_op jit(solution)/shard_map/bring_to_vmem/pallas_call | solution.py:284
  6.6 0.1 collective-permute-start.10
  6.7 1.8 %collective-permute-start.6 = (bf16[2,32,576]{2,1,0:T(8,128)(2,1)S(1)}, bf16[2,32,576]{2,1,0:T(8,128)(2,1)S(1)}, u32[]{:S(2)}, u32[]{:S(2)}) collective-permute-start(bf16[2,32,576]{2,1,0:T(8,128)(2,1)S(1)} %get-tuple-element.25.refs_3_), channel_id=1, source_target_pairs={{0,4},{4,0},{8,12},{12,8},{16,20},{20,16},{24,28},{28,24},{1,5},{5... | collective-permute-start | bytes 221192 | tf_op jit(solution)/shard_map/ppermute | solution.py:18
  8.5 0.1 tile.10
  8.6 0.7 multiply_add_fusion
  9.3 0.8 select_reduce_fusion.1
  10.0 0.0 collective-permute-done.1.refs_0_
  10.1 0.4 collective-permute-start.3
  10.4 0.1 select_reduce_fusion
  10.5 0.1 concatenate.3.table
  10.6 0.9 %collective-permute-done.refs_2_ = bf16[2,32,576]{2,1,0:T(8,128)(2,1)S(1)} collective-permute-done((bf16[2,32,576]{2,1,0:T(8,128)(2,1)}, bf16[2,32,576]{2,1,0:T(8,128)(2,1)S(1)}, u32[]{:S(2)}, u32[]{:S(2)}) %collective-permute-start) | collective-permute-done | bytes 73760 | tf_op jit(solution)/shard_map/ppermute | solution.py:18
  11.5 1.6 %collective-permute-start.5 = (bf16[2,32,576]{2,1,0:T(8,128)(2,1)S(1)}, bf16[2,32,576]{2,1,0:T(8,128)(2,1)S(1)}, u32[]{:S(2)}, u32[]{:S(2)}) collective-permute-start(bf16[2,32,576]{2,1,0:T(8,128)(2,1)S(1)} %collective-permute-done.refs_2_), channel_id=1, source_target_pairs={{0,4},{4,0},{8,12},{12,8},{16,20},{20,16},{24,28},{28,24},{1,5},{5... | collective-permute-start | bytes 221192 | tf_op jit(solution)/shard_map/ppermute | solution.py:18
  13.1 0.0 collective-permute-done.10.refs_11_
  13.1 0.4 collective-permute-start.4
  13.5 1.2 %collective-permute-done.3.refs_4_ = bf16[2,32,576]{2,1,0:T(8,128)(2,1)S(1)} collective-permute-done((bf16[2,32,576]{2,1,0:T(8,128)(2,1)S(1)}, bf16[2,32,576]{2,1,0:T(8,128)(2,1)S(1)}, u32[]{:S(2)}, u32[]{:S(2)}) %collective-permute-start.3) | collective-permute-done | bytes 73760 | tf_op jit(solution)/shard_map/ppermute | solution.py:18
  14.7 0.0 collective-permute-start.9
  14.7 3.1 %bring_to_vmem.3 = (bf16[32,224,512]{2,1,0:T(8,128)(2,1)S(1)}, bf16[32,2,224]{2,1,0:T(2,128)(2,1)S(1)}) custom-call(bf16[32,224,512]{2,1,0:T(8,128)(2,1)} %bitcast.15, bf16[32,2,224]{2,1,0:T(2,128)(2,1)} %refs_1_.2), custom_call_target="tpu_custom_call" | custom-call | bytes 14737408 | tf_op jit(solution)/shard_map/bring_to_vmem/pallas_call | solution.py:284
  17.8 0.0 collective-permute-done.6.refs_7_
  17.8 0.6 collective-permute-start.8
  18.4 0.1 collective-permute-start.14
  18.5 0.4 collective-permute-start.13
  18.9 0.1 collective-permute-start.12
  19.0 0.4 collective-permute-start.11
  19.4 0.0 collective-permute-done.8.refs_9_
  19.4 0.2 collective-permute-done.14.refs_15_
  19.7 0.2 collective-permute-done.13.refs_14_
  19.8 0.4 collective-permute-done.12.refs_13_
  20.2 0.2 collective-permute-done.11.refs_12_
  20.4 1.1 %softmax_weights.1 = bf16[16,512]{1,0:T(8,128)(2,1)S(1)} custom-call(s32[98]{0:T(128)S(1)} %concatenate.3.table, bf16[2,32,576]{2,1,0:T(8,128)(2,1)S(1)} %collective-permute-done.1.refs_0_, bf16[2,32,576]{2,1,0:T(8,128)(2,1)S(1)} %collective-permute-done.2.refs_1_, bf16[2,32,576]{2,1,0:T(8,128)(2,1)S(1)} %collective-permute-done.refs_2_, ...), custom_call_target="tpu_custom_call" | custom-call | tf_op jit(solution)/shard_map/softmax_weights/pallas_call | solution.py:299
  21.4 12.8 %all_to_all.15.refs_16_ = bf16[8,16,512]{2,1,0:T(8,128)(2,1)S(1)} all-to-all(bf16[8,16,512]{2,1,0:T(8,128)(2,1)S(1)} %broadcast_in_dim.57), channel_id=1, replica_groups=mesh['groups'=1,'chip'=8,'core'=2,'tp'=2] {'chip'}, dimensions={0} | all-to-all | bytes 262144 | tf_op jit(solution)/shard_map/all_to_all | solution.py:371
  34.2 0.0 collective-permute-start.15
  34.2 1.3 %collective-permute-done.15.refs_17_ = bf16[8,16,512]{2,1,0:T(8,128)(2,1)S(1)} collective-permute-done((bf16[8,16,512]{2,1,0:T(8,128)(2,1)S(1)}, bf16[8,16,512]{2,1,0:T(8,128)(2,1)S(1)}, u32[]{:S(2)}, u32[]{:S(2)}) %collective-permute-start.15) | collective-permute-done | bytes 131104 | tf_op jit(solution)/shard_map/ppermute | solution.py:13
  35.6 0.0 copy-start.4
  35.6 5.0 %attend_project.1 = (bf16[64,224]{1,0:T(8,128)(2,1)S(1)}, bf16[64,224]{1,0:T(8,128)(2,1)S(1)}, bf16[512,3584]{1,0:T(8,128)(2,1)S(1)}) custom-call(s32[98]{0:T(128)S(1)} %concatenate.3.table, bf16[2,32,576]{2,1,0:T(8,128)(2,1)S(1)} %collective-permute-done.1.refs_0_, bf16[2,32,576]{2,1,0:T(8,128)(2,1)S(1)} %collective-permute-done.2.refs_1_, ...), custom_call_target="tpu_custom_call" | custom-call | bytes 62914560 | tf_op jit(solution)/shard_map/attend_project/pallas_call | solution.py:315
  40.6 1.6 %collective-permute-start.16 = (bf16[64,224]{1,0:T(8,128)(2,1)S(1)}, bf16[64,224]{1,0:T(8,128)(2,1)S(1)}, u32[]{:S(2)}, u32[]{:S(2)}) collective-permute-start(bf16[64,224]{1,0:T(8,128)(2,1)S(1)} %get-tuple-element.36), channel_id=1, source_target_pairs={{0,1},{1,0},{2,3},{3,2},{4,5},{5,4},{6,7},{7,6},{8,9},{9,8},{10,11... | collective-permute-start | bytes 86024 | tf_op jit(solution)/shard_map/ppermute | solution.py:23
  42.1 2.4 %collective-permute-done.16 = bf16[64,224]{1,0:T(8,128)(2,1)S(1)} collective-permute-done((bf16[64,224]{1,0:T(8,128)(2,1)S(1)}, bf16[64,224]{1,0:T(8,128)(2,1)S(1)}, u32[]{:S(2)}, u32[]{:S(2)}) %collective-permute-start.16) | collective-permute-done | bytes 28704 | tf_op jit(solution)/shard_map/ppermute | solution.py:23
  44.6 10.9 %all_to_all.16.same = bf16[8,64,224]{2,1,0:T(8,128)(2,1)S(1)} all-to-all(bf16[8,64,224]{2,1,0:T(8,128)(2,1)S(1)} %broadcast_in_dim.58), channel_id=1, replica_groups=mesh['groups'=1,'chip'=8,'core'=2,'tp'=2] {'chip'}, dimensions={0} | all-to-all | bytes 458752 | tf_op jit(solution)/shard_map/all_to_all | solution.py:371
  55.5 1.5 %collective-permute-done.17.other = bf16[8,64,224]{2,1,0:T(8,128)(2,1)S(1)} collective-permute-done((bf16[8,64,224]{2,1,0:T(8,128)(2,1)S(1)}, bf16[8,64,224]{2,1,0:T(8,128)(2,1)S(1)}, u32[]{:S(2)}, u32[]{:S(2)}) %collective-permute-start.17) | collective-permute-done | bytes 229408 | tf_op jit(solution)/shard_map/ppermute | solution.py:13
  57.1 3.7 %expert_mlp.1 = (bf16[16,64,112]{2,1,0:T(8,128)(2,1)S(1)}, bf16[16,64,112]{2,1,0:T(8,128)(2,1)S(1)}, bf16[64,112]{1,0:T(8,128)(2,1)S(1)}) custom-call(s32[98]{0:T(128)S(1)} %concatenate.3.table, bf16[8,64,224]{2,1,0:T(8,128)(2,1)S(1)} %all_to_all.16.same, bf16[8,64,224]{2,1,0:T(8,128)(2,1)S(1)} %collective-permute-done.17.other, f32[28,128]{1,0:T(8,128)S(1)} %bitcast.12, ...), custom_call_target="tpu_custom_call" | custom-call | tf_op jit(solution)/shard_map/expert_mlp/pallas_call | solution.py:346
  60.8 0.3 collective-permute-start.18
  61.1 1.3 %collective-permute-done.18 = bf16[16,64,112]{2,1,0:T(8,128)(2,1)S(1)} collective-permute-done((bf16[16,64,112]{2,1,0:T(8,128)(2,1)S(1)}, bf16[16,64,112]{2,1,0:T(8,128)(2,1)S(1)}, u32[]{:S(2)}, u32[]{:S(2)}) %collective-permute-start.18) | collective-permute-done | bytes 229408 | tf_op jit(solution)/shard_map/ppermute | solution.py:13
  62.4 0.1 add_convert_fusion
  62.4 14.5 %all_to_all.17 = bf16[16,64,112]{2,1,0:T(8,128)(2,1)S(1)} all-to-all(bf16[16,64,112]{2,1,0:T(8,128)(2,1)S(1)} %add_convert_fusion), channel_id=1, replica_groups=mesh['groups'=1,'chip'=8,'core'=2,'tp'=2] {'chip','tp'}, dimensions={0} | all-to-all | bytes 458752 | tf_op jit(solution)/shard_map/all_to_all | solution.py:563
  77.0 0.1 convert_reduce_fusion
  77.1 0.6 add_convert_fusion.2
  (21 shorter events, 0.1 us)
Async XLA Ops:
  0.0 10.0 %collective-permute-start.1 = (bf16[2,32,576]{2,1,0:T(8,128)(2,1)}, bf16[2,32,576]{2,1,0:T(8,128)(2,1)S(1)}, u32[]{:S(2)}, u32[]{:S(2)}) collective-permute-start(bf16[2,32,576]{2,1,0:T(8,128)(2,1)} %refs_0_.1), channel_id=1, source_target_pairs={{0,24},{4,28},{8,16},{12,20},{16,8},{20,12},{24,0},{28,4},{1,25},{... | collective-permute-start | bytes 221192 | tf_op jit(solution)/shard_map/ppermute | solution.py:18
  5.0 6.4 %collective-permute-start = (bf16[2,32,576]{2,1,0:T(8,128)(2,1)}, bf16[2,32,576]{2,1,0:T(8,128)(2,1)S(1)}, u32[]{:S(2)}, u32[]{:S(2)}) collective-permute-start(bf16[2,32,576]{2,1,0:T(8,128)(2,1)} %refs_0_.1), channel_id=1, source_target_pairs={{0,8},{4,12},{8,0},{12,4},{16,24},{20,28},{24,16},{28,20},{1,9},{5... | collective-permute-start | bytes 221192 | tf_op jit(solution)/shard_map/ppermute | solution.py:18
  5.1 6.4 %collective-permute-start.2 = (bf16[2,32,576]{2,1,0:T(8,128)(2,1)}, bf16[2,32,576]{2,1,0:T(8,128)(2,1)S(1)}, u32[]{:S(2)}, u32[]{:S(2)}) collective-permute-start(bf16[2,32,576]{2,1,0:T(8,128)(2,1)} %refs_0_.1), channel_id=1, source_target_pairs={{0,16},{4,20},{8,24},{12,28},{16,0},{20,4},{24,8},{28,12},{1,17},{... | collective-permute-start | bytes 221192 | tf_op jit(solution)/shard_map/ppermute | solution.py:18
  6.6 6.5 %collective-permute-start.10 = (bf16[2,32,576]{2,1,0:T(8,128)(2,1)S(1)}, bf16[2,32,576]{2,1,0:T(8,128)(2,1)S(1)}, u32[]{:S(2)}, u32[]{:S(2)}) collective-permute-start(bf16[2,32,576]{2,1,0:T(8,128)(2,1)S(1)} %get-tuple-element.25.refs_3_), channel_id=1, source_target_pairs={{0,2},{2,0},{1,3},{3,1},{4,6},{6,4},{5,7},{7,5},{8,10},{10,8},{9,1... | collective-permute-start | bytes 221192 | tf_op jit(solution)/shard_map/ppermute | solution.py:13
  6.7 11.1 %collective-permute-start.6 = (bf16[2,32,576]{2,1,0:T(8,128)(2,1)S(1)}, bf16[2,32,576]{2,1,0:T(8,128)(2,1)S(1)}, u32[]{:S(2)}, u32[]{:S(2)}) collective-permute-start(bf16[2,32,576]{2,1,0:T(8,128)(2,1)S(1)} %get-tuple-element.25.refs_3_), channel_id=1, source_target_pairs={{0,4},{4,0},{8,12},{12,8},{16,20},{20,16},{24,28},{28,24},{1,5},{5... | collective-permute-start | bytes 221192 | tf_op jit(solution)/shard_map/ppermute | solution.py:18
  10.1 4.6 %collective-permute-start.3 = (bf16[2,32,576]{2,1,0:T(8,128)(2,1)S(1)}, bf16[2,32,576]{2,1,0:T(8,128)(2,1)S(1)}, u32[]{:S(2)}, u32[]{:S(2)}) collective-permute-start(bf16[2,32,576]{2,1,0:T(8,128)(2,1)S(1)} %collective-permute-done.1.refs_0_), channel_id=1, source_target_pairs={{0,4},{4,0},{8,12},{12,8},{16,20},{20,16},{24,28},{28,24},{1,5},{5... | collective-permute-start | bytes 221192 | tf_op jit(solution)/shard_map/ppermute | solution.py:18
  11.5 6.9 %collective-permute-start.7 = (bf16[2,32,576]{2,1,0:T(8,128)(2,1)S(1)}, bf16[2,32,576]{2,1,0:T(8,128)(2,1)S(1)}, u32[]{:S(2)}, u32[]{:S(2)}) collective-permute-start(bf16[2,32,576]{2,1,0:T(8,128)(2,1)S(1)} %collective-permute-done.1.refs_0_), channel_id=1, source_target_pairs={{0,2},{2,0},{1,3},{3,1},{4,6},{6,4},{5,7},{7,5},{8,10},{10,8},{9,1... | collective-permute-start | bytes 221192 | tf_op jit(solution)/shard_map/ppermute | solution.py:13
  11.5 7.0 %collective-permute-start.5 = (bf16[2,32,576]{2,1,0:T(8,128)(2,1)S(1)}, bf16[2,32,576]{2,1,0:T(8,128)(2,1)S(1)}, u32[]{:S(2)}, u32[]{:S(2)}) collective-permute-start(bf16[2,32,576]{2,1,0:T(8,128)(2,1)S(1)} %collective-permute-done.refs_2_), channel_id=1, source_target_pairs={{0,4},{4,0},{8,12},{12,8},{16,20},{20,16},{24,28},{28,24},{1,5},{5... | collective-permute-start | bytes 221192 | tf_op jit(solution)/shard_map/ppermute | solution.py:18
  13.1 5.8 %collective-permute-start.4 = (bf16[2,32,576]{2,1,0:T(8,128)(2,1)S(1)}, bf16[2,32,576]{2,1,0:T(8,128)(2,1)S(1)}, u32[]{:S(2)}, u32[]{:S(2)}) collective-permute-start(bf16[2,32,576]{2,1,0:T(8,128)(2,1)S(1)} %collective-permute-done.2.refs_1_), channel_id=1, source_target_pairs={{0,4},{4,0},{8,12},{12,8},{16,20},{20,16},{24,28},{28,24},{1,5},{5... | collective-permute-start | bytes 221192 | tf_op jit(solution)/shard_map/ppermute | solution.py:18
  14.7 4.3 %collective-permute-start.9 = (bf16[2,32,576]{2,1,0:T(8,128)(2,1)S(1)}, bf16[2,32,576]{2,1,0:T(8,128)(2,1)S(1)}, u32[]{:S(2)}, u32[]{:S(2)}) collective-permute-start(bf16[2,32,576]{2,1,0:T(8,128)(2,1)S(1)} %collective-permute-done.refs_2_), channel_id=1, source_target_pairs={{0,2},{2,0},{1,3},{3,1},{4,6},{6,4},{5,7},{7,5},{8,10},{10,8},{9,1... | collective-permute-start | bytes 221192 | tf_op jit(solution)/shard_map/ppermute | solution.py:13
  17.8 1.6 %collective-permute-start.8 = (bf16[2,32,576]{2,1,0:T(8,128)(2,1)S(1)}, bf16[2,32,576]{2,1,0:T(8,128)(2,1)S(1)}, u32[]{:S(2)}, u32[]{:S(2)}) collective-permute-start(bf16[2,32,576]{2,1,0:T(8,128)(2,1)S(1)} %collective-permute-done.2.refs_1_), channel_id=1, source_target_pairs={{0,2},{2,0},{1,3},{3,1},{4,6},{6,4},{5,7},{7,5},{8,10},{10,8},{9,1... | collective-permute-start | bytes 221192 | tf_op jit(solution)/shard_map/ppermute | solution.py:13
  18.4 1.3 %collective-permute-start.14 = (bf16[2,32,576]{2,1,0:T(8,128)(2,1)S(1)}, bf16[2,32,576]{2,1,0:T(8,128)(2,1)S(1)}, u32[]{:S(2)}, u32[]{:S(2)}) collective-permute-start(bf16[2,32,576]{2,1,0:T(8,128)(2,1)S(1)} %collective-permute-done.6.refs_7_), channel_id=1, source_target_pairs={{0,2},{2,0},{1,3},{3,1},{4,6},{6,4},{5,7},{7,5},{8,10},{10,8},{9,1... | collective-permute-start | bytes 221192 | tf_op jit(solution)/shard_map/ppermute | solution.py:13
  18.5 1.3 %collective-permute-start.13 = (bf16[2,32,576]{2,1,0:T(8,128)(2,1)S(1)}, bf16[2,32,576]{2,1,0:T(8,128)(2,1)S(1)}, u32[]{:S(2)}, u32[]{:S(2)}) collective-permute-start(bf16[2,32,576]{2,1,0:T(8,128)(2,1)S(1)} %collective-permute-done.5.refs_6_), channel_id=1, source_target_pairs={{0,2},{2,0},{1,3},{3,1},{4,6},{6,4},{5,7},{7,5},{8,10},{10,8},{9,1... | collective-permute-start | bytes 221192 | tf_op jit(solution)/shard_map/ppermute | solution.py:13
  18.9 1.3 %collective-permute-start.12 = (bf16[2,32,576]{2,1,0:T(8,128)(2,1)S(1)}, bf16[2,32,576]{2,1,0:T(8,128)(2,1)S(1)}, u32[]{:S(2)}, u32[]{:S(2)}) collective-permute-start(bf16[2,32,576]{2,1,0:T(8,128)(2,1)S(1)} %collective-permute-done.4.refs_5_), channel_id=1, source_target_pairs={{0,2},{2,0},{1,3},{3,1},{4,6},{6,4},{5,7},{7,5},{8,10},{10,8},{9,1... | collective-permute-start | bytes 221192 | tf_op jit(solution)/shard_map/ppermute | solution.py:13
  19.0 1.3 %collective-permute-start.11 = (bf16[2,32,576]{2,1,0:T(8,128)(2,1)S(1)}, bf16[2,32,576]{2,1,0:T(8,128)(2,1)S(1)}, u32[]{:S(2)}, u32[]{:S(2)}) collective-permute-start(bf16[2,32,576]{2,1,0:T(8,128)(2,1)S(1)} %collective-permute-done.3.refs_4_), channel_id=1, source_target_pairs={{0,2},{2,0},{1,3},{3,1},{4,6},{6,4},{5,7},{7,5},{8,10},{10,8},{9,1... | collective-permute-start | bytes 221192 | tf_op jit(solution)/shard_map/ppermute | solution.py:13
  34.2 1.3 %collective-permute-start.15 = (bf16[8,16,512]{2,1,0:T(8,128)(2,1)S(1)}, bf16[8,16,512]{2,1,0:T(8,128)(2,1)S(1)}, u32[]{:S(2)}, u32[]{:S(2)}) collective-permute-start(bf16[8,16,512]{2,1,0:T(8,128)(2,1)S(1)} %all_to_all.15.refs_16_), channel_id=1, source_target_pairs={{0,2},{2,0},{1,3},{3,1},{4,6},{6,4},{5,7},{7,5},{8,10},{10,8},{9,1... | collective-permute-start | bytes 393224 | tf_op jit(solution)/shard_map/ppermute | solution.py:13
  35.6 21.5 %copy-start = (bf16[1,3584,512]{2,1,0:T(8,128)(2,1)S(1)}, bf16[1,3584,512]{2,1,0:T(8,128)(2,1)}, u32[]{:S(2)}) copy-start(bf16[1,3584,512]{2,1,0:T(8,128)(2,1)} %param.21) | copy-start | bytes 11010052
  35.6 21.5 %copy-start.1 = (bf16[1,3584,512]{2,1,0:T(8,128)(2,1)S(1)}, bf16[1,3584,512]{2,1,0:T(8,128)(2,1)}, u32[]{:S(2)}) copy-start(bf16[1,3584,512]{2,1,0:T(8,128)(2,1)} %param.22) | copy-start | bytes 11010052
  35.6 21.5 %copy-start.2 = (f32[3584]{0:T(1024)S(1)}, f32[3584]{0:T(1024)}, u32[]{:S(2)}) copy-start(f32[3584]{0:T(1024)} %param.20) | copy-start | bytes 43012
  35.6 21.5 %copy-start.3 = (s32[32,2,8]{0,2,1:T(8,128)S(1)}, s32[32,2,8]{0,2,1:T(8,128)}, u32[]{:S(2)}) copy-start(s32[32,2,8]{0,2,1:T(8,128)} %param.24) | copy-start | bytes 6148
  35.6 21.5 %copy-start.4 = (f32[32,2,8]{0,2,1:T(8,128)S(1)}, f32[32,2,8]{0,2,1:T(8,128)}, u32[]{:S(2)}) copy-start(f32[32,2,8]{0,2,1:T(8,128)} %param.25) | copy-start | bytes 6148
  40.6 4.0 %collective-permute-start.16 = (bf16[64,224]{1,0:T(8,128)(2,1)S(1)}, bf16[64,224]{1,0:T(8,128)(2,1)S(1)}, u32[]{:S(2)}, u32[]{:S(2)}) collective-permute-start(bf16[64,224]{1,0:T(8,128)(2,1)S(1)} %get-tuple-element.36), channel_id=1, source_target_pairs={{0,1},{1,0},{2,3},{3,2},{4,5},{5,4},{6,7},{7,6},{8,9},{9,8},{10,11... | collective-permute-start | bytes 86024 | tf_op jit(solution)/shard_map/ppermute | solution.py:23
  55.5 1.5 %collective-permute-start.17 = (bf16[8,64,224]{2,1,0:T(8,128)(2,1)S(1)}, bf16[8,64,224]{2,1,0:T(8,128)(2,1)S(1)}, u32[]{:S(2)}, u32[]{:S(2)}) collective-permute-start(bf16[8,64,224]{2,1,0:T(8,128)(2,1)S(1)} %all_to_all.16.same), channel_id=1, source_target_pairs={{0,2},{2,0},{1,3},{3,1},{4,6},{6,4},{5,7},{7,5},{8,10},{10,8},{9,1... | collective-permute-start | bytes 688136 | tf_op jit(solution)/shard_map/ppermute | solution.py:13
  60.8 1.6 %collective-permute-start.18 = (bf16[16,64,112]{2,1,0:T(8,128)(2,1)S(1)}, bf16[16,64,112]{2,1,0:T(8,128)(2,1)S(1)}, u32[]{:S(2)}, u32[]{:S(2)}) collective-permute-start(bf16[16,64,112]{2,1,0:T(8,128)(2,1)S(1)} %get-tuple-element.40), channel_id=1, source_target_pairs={{0,2},{2,0},{1,3},{3,1},{4,6},{6,4},{5,7},{7,5},{8,10},{10,8},{9,1... | collective-permute-start | bytes 688136 | tf_op jit(solution)/shard_map/ppermute | solution.py:13
